TPU v7x, 256 devices: a whole 4x4x8 slice. The times are simulated.
256 devices in a mesh: head: 16 (over y_hi, z), blk: 16 (over x, y_lo, core).
Axes of the slice: x: 4, y: 4 (y_hi: 2, y_lo: 2; y = y_hi * 2 + y_lo), z: 8, core: 2. Of those that a mesh axis runs over, the one named last changes fastest.
Arguments:
- hidden: bfloat16 [12288, 3072], P(('blk', 'head')), may hold values from -6 to 6
- cotangent: bfloat16 [12288, 3072], P(('blk', 'head')), may hold values from -6 to 6
- step_index: int32 [1], replicated, may hold values from 0 to 31
- mod_table: float32 [32, 3, 3072], replicated, may hold values from -3 to 3
- w_qkv: bfloat16 [3072, 16, 384], P(None, 'head'), may hold values from -0.109375 to 0.109375
- qk_gains: float32 [2, 128], replicated, may hold values from 0.6 to 2.4
- w_out: bfloat16 [16, 128, 3072], P('head'), may hold values from -0.125 to 0.125
- tile_pairs: int32 [16, 3], replicated, may hold values from -1 to 15, as said below
- tile_owner: int32 [16], replicated, may hold values from 0 to 15, each once
Outputs:
- result: bfloat16 [12288, 3072], P(('blk', 'head'))
- grad_hidden: bfloat16 [12288, 3072], P(('blk', 'head'))
Inputs may be any that keep to these rules, and one draw needn't show every extreme that they name: `tile_pairs`: row t lists first t itself, then none, one or both of (t - 1) mod 16 and (t + 1) mod 16, each at most once; unused slots hold -1 and come last.
All inputs are finite; a program needn't handle non-finite values.
Results may differ from a plain program's by a relative error of at most 0.024.
Values may be sent and summed in bfloat16 or wider, within the bound.
A program may use at most 128 MiB of HBM per device.

v0:
```python
import jax
import jax.numpy as jnp
from jax import lax
from jax.sharding import PartitionSpec as P

TILE = 768
TILES_BLK = 1


EPS = 1e-06
NEG = -1e30


def rounded(values):
    return lax.optimization_barrier(values.astype(jnp.bfloat16)).astype(jnp.float32)


def layer_norm(rows):
    center = rows - jnp.mean(rows, axis=-1, keepdims=True)
    spread = jnp.mean(center * center, axis=-1, keepdims=True)
    return center * lax.rsqrt(spread + EPS)


def modulate(rows, shift, scale):
    return layer_norm(rows) * (1.0 + scale) + shift


def rms_gain(source, gain):
    return source * lax.rsqrt(jnp.mean(source * source, axis=-1, keepdims=True) + EPS) * gain


def inverse_positions(tile_owner):
    count = tile_owner.shape[0]
    places = jnp.arange(count, dtype=jnp.int32)
    match = tile_owner[None, :] == places[:, None]
    return jnp.sum(jnp.where(match, places[None, :], 0), axis=1)


def listed_keys(keys, values, listed, inverse, tile_rows):
    key_parts, value_parts, flags = ([], [], [])
    for number in range(listed.shape[0]):
        entry = listed[number]
        begin = inverse[jnp.maximum(entry, 0)] * tile_rows
        key_parts.append(lax.dynamic_slice_in_dim(keys, begin, tile_rows, 0))
        value_parts.append(lax.dynamic_slice_in_dim(values, begin, tile_rows, 0))
        flags.append(jnp.broadcast_to(entry >= 0, (tile_rows,)))
    return (
        jnp.concatenate(key_parts, 0),
        jnp.concatenate(value_parts, 0),
        jnp.concatenate(flags, 0),
    )


def tile_attention(query, keys, values, valid, factor):
    scores = jnp.einsum("qhd,khd->hqk", query, keys, preferred_element_type=jnp.float32) * factor
    scores = jnp.where(valid[None, None, :], scores, NEG)
    expos = jnp.exp(scores)
    total = jnp.sum(expos, axis=-1)
    prob_low = (expos / total[..., None]).astype(jnp.bfloat16)
    attended = jnp.einsum("hqk,khd->qhd", prob_low, values, preferred_element_type=jnp.float32)
    return (attended.astype(jnp.bfloat16), total)


def score_terms(query, keys, values, valid, d_out, total, delta, factor):
    scores = jnp.einsum("qhd,khd->hqk", query, keys, preferred_element_type=jnp.float32) * factor
    scores = jnp.where(valid[None, None, :], scores, NEG)
    prob = jnp.exp(scores) / total[..., None]
    d_prob = jnp.einsum("qhd,khd->hqk", d_out, values, preferred_element_type=jnp.float32)
    d_score = (prob * (d_prob - delta[..., None])).astype(jnp.bfloat16)
    return (prob.astype(jnp.bfloat16), d_score)


def key_terms(query, d_out, prob_low, d_score, factor):
    d_keys = jnp.einsum("hqk,qhd->khd", d_score, query, preferred_element_type=jnp.float32) * factor
    d_values = jnp.einsum("hqk,qhd->khd", prob_low, d_out, preferred_element_type=jnp.float32)
    return jnp.concatenate([d_keys, d_values], -1)


def per_device(
    hidden, cotangent, step_index, mod_table, w_qkv, qk_gains, w_out, tile_pairs, tile_owner
):
    heads_local = w_qkv.shape[1]
    head_size = qk_gains.shape[1]
    width = hidden.shape[1]
    factor = head_size ** (-0.5)
    slab_rows = TILE * TILES_BLK
    tile_count = tile_owner.shape[0]
    here = lax.axis_index("blk")
    mods = lax.dynamic_index_in_dim(mod_table, step_index[0], 0, keepdims=False)
    shift, scale, gate = (mods[0], mods[1], mods[2])

    def modulate_rows(rows):
        return modulate(rows, shift, scale)

    def query_norm(source):
        return rms_gain(source, qk_gains[0])

    def keys_norm(source):
        return rms_gain(source, qk_gains[1])

    hidden_wide = hidden.astype(jnp.float32)
    modulated = modulate_rows(hidden_wide).astype(jnp.bfloat16)
    w_flat = w_qkv.reshape(width, heads_local * 3 * head_size)
    w_out_flat = w_out.reshape(heads_local * head_size, width)
    projected = jnp.dot(
        lax.all_gather(modulated, "head", axis=0, tiled=True),
        w_flat,
        preferred_element_type=jnp.float32,
    )
    projected = projected.reshape(slab_rows, heads_local, 3 * head_size)
    raw_query = projected[..., :head_size]
    raw_keys = projected[..., head_size : 2 * head_size]
    query = query_norm(raw_query).astype(jnp.bfloat16)
    keys = keys_norm(raw_keys).astype(jnp.bfloat16)
    values = projected[..., 2 * head_size :].astype(jnp.bfloat16)
    all_keys, all_values = (
        lax.all_gather(keys, "blk", axis=0, tiled=True),
        lax.all_gather(values, "blk", axis=0, tiled=True),
    )
    inverse = inverse_positions(tile_owner)
    out_parts, total_parts, listings = ([], [], [])
    local = 0
    position = here * TILES_BLK + local
    listed = tile_pairs[tile_owner[position]]
    chosen_keys, chosen_values, valid = listed_keys(all_keys, all_values, listed, inverse, TILE)
    attended_tile, total = tile_attention(query, chosen_keys, chosen_values, valid, factor)
    out_parts.append(attended_tile)
    total_parts.append(total)
    listings.append((listed, chosen_keys, chosen_values, valid))
    attended = out_parts[0]
    total_all = total_parts[0]
    attended_flat = attended.reshape(slab_rows, heads_local * head_size)
    rows = attended_flat
    proj = lax.psum_scatter(
        jnp.dot(rows, w_out_flat, preferred_element_type=jnp.float32).astype(jnp.bfloat16),
        "head",
        scatter_dimension=0,
        tiled=True,
    ).astype(jnp.float32)
    result = (hidden_wide + gate * proj).astype(jnp.bfloat16)
    d_proj = (
        lax.all_gather(cotangent, "head", axis=0, tiled=True).astype(jnp.float32) * gate
    ).astype(jnp.bfloat16)
    d_flat = lax.dot_general(
        d_proj, w_out_flat, (((1,), (1,)), ((), ())), preferred_element_type=jnp.float32
    )
    d_attended = d_flat.astype(jnp.bfloat16).reshape(slab_rows, heads_local, head_size)
    delta_all = jnp.sum(d_attended.astype(jnp.float32) * attended.astype(jnp.float32), axis=-1).T
    local = 0
    listed, chosen_keys, chosen_values, valid = listings[local]
    prob_low, d_score = score_terms(
        query, chosen_keys, chosen_values, valid, d_attended, total_all, delta_all, factor
    )
    query_grads = (
        jnp.einsum("hqk,khd->qhd", d_score, chosen_keys, preferred_element_type=jnp.float32)
        * factor
    )
    sent_query, sent_grad, sent_total, sent_delta = (
        lax.all_gather(query, "blk", axis=0, tiled=True),
        lax.all_gather(d_attended, "blk", axis=0, tiled=True),
        lax.all_gather(total_all.astype(jnp.bfloat16), "blk", axis=1, tiled=True).astype(
            total_all.dtype
        ),
        lax.all_gather(delta_all.astype(jnp.bfloat16), "blk", axis=1, tiled=True).astype(
            delta_all.dtype
        ),
    )
    local = 0
    tile = tile_owner[here * TILES_BLK + local]
    pieces = []
    slabs = []
    for offset in (0, tile_count - 1, 1):
        source = (tile + offset) % tile_count
        flagged = jnp.any(tile_pairs[source] == tile)
        valid = jnp.broadcast_to(flagged, (TILE,))
        begin = inverse[source] * TILE
        source_query = lax.dynamic_slice_in_dim(sent_query, begin, TILE, 0)
        source_grad = lax.dynamic_slice_in_dim(sent_grad, begin, TILE, 0)
        prob_low, d_score = score_terms(
            source_query,
            keys,
            values,
            valid,
            source_grad,
            lax.dynamic_slice_in_dim(sent_total, begin, TILE, 1),
            lax.dynamic_slice_in_dim(sent_delta, begin, TILE, 1),
            factor,
        )
        pieces.append(key_terms(source_query, source_grad, prob_low, d_score, factor))
        slabs.append(inverse[source] // TILES_BLK)
    combined = jnp.zeros_like(pieces[0])
    for first in range(len(pieces)):
        grouped = jnp.zeros_like(pieces[0])
        for second in range(len(pieces)):
            grouped = grouped + jnp.where(slabs[second] == slabs[first], pieces[second], 0.0)
        leading = jnp.array(True)
        for earlier in range(first):
            leading = jnp.logical_and(leading, slabs[earlier] != slabs[first])
        combined = combined + jnp.where(leading, rounded(grouped), 0.0)
    _, pull_query = jax.vjp(query_norm, raw_query)
    (d_raw_query,) = pull_query(query_grads)
    _, pull_keys = jax.vjp(keys_norm, raw_keys)
    (d_raw_keys,) = pull_keys(combined[..., :head_size])
    d_projected = jnp.concatenate([d_raw_query, d_raw_keys, combined[..., head_size:]], -1)
    d_projected = d_projected.astype(jnp.bfloat16).reshape(slab_rows, heads_local * 3 * head_size)
    rows = d_projected
    d_modulated = lax.psum_scatter(
        lax.dot_general(
            rows, w_flat, (((1,), (1,)), ((), ())), preferred_element_type=jnp.float32
        ).astype(jnp.bfloat16),
        "head",
        scatter_dimension=0,
        tiled=True,
    ).astype(jnp.float32)
    _, pull_rows = jax.vjp(modulate_rows, hidden_wide)
    (d_input,) = pull_rows(d_modulated)
    grad_hidden = (cotangent.astype(jnp.float32) + d_input).astype(jnp.bfloat16)
    return (result, grad_hidden)


def solution(mesh):
    in_specs = (
        P(("blk", "head"), None),
        P(("blk", "head"), None),
        P(),
        P(),
        P(None, "head", None),
        P(),
        P("head", None, None),
        P(),
        P(),
    )
    out_specs = (P(("blk", "head"), None), P(("blk", "head"), None))
    return jax.shard_map(
        per_device, mesh=mesh, in_specs=in_specs, out_specs=out_specs, check_vma=False
    )
```

profile of v0, /device:TPU:9, one launch (start us, length us, event | category | flops | bytes accessed | tf_op | source)
XLA Modules:
  0.0 861.7 jit_solution(16126996644440111657)
XLA Ops:
  8.0 1.1 convert_reduce_fusion
  9.1 1.2 fusion.39
  10.4 0.5 copy-done.29
  10.9 1.6 constant_dynamic-slice_fusion
  12.5 1.8 fusion.42
  14.4 1.3 slice_bitcast_fusion.1
  15.7 101.5 %all-gather.12.cloned.1.call-done = bf16[768,3072]{1,0:T(8,128)(2,1)} async-done(((bf16[48,3072]{1,0:T(8,128)(2,1)}), bf16[768,3072]{1,0:T(8,128)(2,1)}) %all-gather.12.cloned.1.call-update) | async-done | bytes 4718608 | tf_op jit(solution)/shard_map/all_gather | solution.py:106
  117.3 4.4 fusion.8
  121.8 0.6 copy-done.18
  122.4 0.6 copy-done.17
  122.9 0.9 multiply_convert_fusion.9
  123.9 0.7 slice.94
  124.7 0.5 all-gather.18.cloned.1.call-update
  125.2 0.5 all-gather.20.cloned.1.call-update
  125.8 1.3 dynamic_slice.96
  132.0 0.8 constant_dynamic-slice_fusion.10
  132.8 0.5 fusion.117
  135.2 0.8 select_reduce_fusion
  136.0 0.7 fusion.118
  140.4 0.6 pad_add_fusion
  141.0 22.0 %all-gather.16.cloned.1.call-done = bf16[12288,1,128]{0,2,1:T(8,128)(2,1)} async-done(((bf16[768,1,128]{0,2,1:T(8,128)(2,1)}), bf16[12288,1,128]{0,2,1:T(8,128)(2,1)}) %all-gather.16.cloned.1.call-update) | async-done | bytes 3145744 | tf_op jit(solution)/shard_map/all_gather | solution.py:117
  163.0 2.0 constant_dynamic-slice_fusion.6
  164.9 38.5 %all-gather.14.cloned.1.call-done = bf16[12288,1,128]{0,2,1:T(8,128)(2,1)} async-done(((bf16[768,1,128]{0,2,1:T(8,128)(2,1)}), bf16[12288,1,128]{0,2,1:T(8,128)(2,1)}) %all-gather.14.cloned.1.call-update) | async-done | bytes 3145744 | tf_op jit(solution)/shard_map/all_gather | solution.py:118
  203.5 1.2 constant_dynamic-slice_fusion.9
  204.7 3.2 fusion.119
  207.9 0.5 copy-done.27
  208.4 2.3 copy-done.31
  210.7 2.1 fusion.29
  212.9 93.0 %all-gather.18.cloned.1.call-done = bf16[768,3072]{1,0:T(8,128)(2,1)} async-done(((bf16[48,3072]{1,0:T(8,128)(2,1)}), bf16[768,3072]{1,0:T(8,128)(2,1)}) %all-gather.18.cloned.1.call-update) | async-done | bytes 4718608 | tf_op jit(solution)/shard_map/all_gather | solution.py:142
  305.9 5.6 fusion.52
  325.4 2.3 fusion.108
  327.7 1.2 broadcast_multiply_fusion
  328.9 0.7 convert_element_type.192
  329.6 21.2 %all-gather.3 = bf16[16,1,768]{2,1,0:T(2,128)(2,1)S(1)} all-gather(bf16[1,1,768]{2,1,0:T(2,128)(2,1)S(1)} %reshape.674), channel_id=2, replica_groups=mesh['head'=16,'blk'=16] {'blk'}, dimensions={0}, use_global_device_ids=true | all-gather | bytes 26112 | tf_op jit(solution)/shard_map/all_gather | solution.py:161
  350.9 0.7 convert_element_type.195
  351.6 19.2 %all-gather.4 = bf16[16,1,768]{2,1,0:T(2,128)(2,1)S(1)} all-gather(bf16[1,1,768]{2,1,0:T(2,128)(2,1)S(1)} %reshape.676), channel_id=4, replica_groups=mesh['head'=16,'blk'=16] {'blk'}, dimensions={0}, use_global_device_ids=true | all-gather | bytes 26112 | tf_op jit(solution)/shard_map/all_gather | solution.py:164
  370.8 0.7 fusion.116
  371.5 0.7 fusion.115
  372.2 3.9 exponential_divide_fusion.2
  376.1 3.6 exponential_divide_fusion.1
  379.7 3.6 exponential_divide_fusion
  383.3 4.2 all-gather.22.cloned.1.call-done
  387.5 2.9 convolution_bitcast_fusion.2
  390.4 3.3 fusion.19
  393.7 2.9 convolution_bitcast_fusion.1
  396.6 3.3 fusion.17
  399.9 2.9 convolution_bitcast_fusion
  402.8 3.4 fusion.15
  406.2 2.0 add_convert_fusion.2
  408.5 0.1 add_convert_fusion
  408.6 0.2 select_add_fusion
  408.8 0.9 copy-done.8
  409.7 0.7 fusion.54
  410.4 7.4 multiply_reduce_fusion.1
  417.8 0.7 multiply_multiply_fusion
  418.5 1.3 fusion.56
  419.8 5.4 convolution_convert_fusion
  425.3 1.1 copy-done.10
  426.4 3.6 convolution_convert_fusion.1
  430.0 205.5 %reduce-scatter.5.cloned.1.call-done = bf16[48,3072]{1,0:T(8,128)(2,1)} async-done(((bf16[768,3072]{1,0:T(8,128)(2,1)}), bf16[48,3072]{1,0:T(8,128)(2,1)}) %reduce-scatter.5.cloned.1.call-update) | async-done | bytes 294928 | tf_op jit(solution)/shard_map/reduce_scatter | solution.py:207
  635.4 1.2 fusion.43
  636.7 1.3 fusion.53
  638.0 214.7 %reduce-scatter.3.cloned.1.call-done = bf16[48,3072]{1,0:T(8,128)(2,1)} async-done(((bf16[768,3072]{1,0:T(8,128)(2,1)}), bf16[48,3072]{1,0:T(8,128)(2,1)}) %reduce-scatter.3.cloned.1.call-update) | async-done | bytes 294928 | tf_op jit(solution)/shard_map/reduce_scatter | solution.py:134
  852.7 2.2 add_convert_fusion.3
  (86 shorter events, 1.1 us)
Async XLA Ops:
  7.2 110.1 %copy-start = (bf16[3072,1,384]{2,0,1:T(8,128)(2,1)S(1)}, bf16[3072,1,384]{2,0,1:T(8,128)(2,1)}, u32[]{:S(2)}) copy-start(bf16[3072,1,384]{2,0,1:T(8,128)(2,1)} %param.13) | copy-start | bytes 7077892
  7.2 110.1 %all-gather.12.cloned.1.call-start = ((), (), s32[]{:S(2)}) async-start(), calls=%async_computation.2 | async-start | bytes 5013504 | tf_op jit(solution)/shard_map/all_gather | solution.py:106
  9.1 6.6 copy-start.20
  10.4 0.5 copy-start.29
  10.4 5.4 copy-start.23
  14.4 148.6 %all-gather.16.cloned.1.call-start = ((), (), s32[]{:S(2)}) async-start(), calls=%async_computation.4 | async-start | bytes 3342336 | tf_op jit(solution)/shard_map/all_gather | solution.py:117
  117.3 5.6 copy-start.22
  117.3 5.6 copy-start.28
  121.8 0.6 copy-start.18
  121.8 2.0 copy-start.19
  122.3 0.6 copy-start.17
  123.8 79.7 %all-gather.14.cloned.1.call-start = ((), (), s32[]{:S(2)}) async-start(), calls=%async_computation.3 | async-start | bytes 3342336 | tf_op jit(solution)/shard_map/all_gather | solution.py:118
  124.6 181.3 %all-gather.18.cloned.1.call-start = ((), (), s32[]{:S(2)}) async-start(), calls=%async_computation.6 | async-start | bytes 5013504 | tf_op jit(solution)/shard_map/all_gather | solution.py:142
  125.2 247.0 %all-gather.20.cloned.1.call-start = ((), (), s32[]{:S(2)}) async-start(), calls=%async_computation.7 | async-start | bytes 3342336 | tf_op jit(solution)/shard_map/all_gather | solution.py:159
  125.8 261.7 %all-gather.22.cloned.1.call-start = ((), (), s32[]{:S(2)}) async-start(), calls=%async_computation.9 | async-start | bytes 3342336 | tf_op jit(solution)/shard_map/all_gather | solution.py:160
  204.6 3.2 copy-start.13
  204.6 3.2 copy-start.14
  204.6 3.2 copy-start.15
  207.9 0.6 copy-start.27
  207.9 2.9 copy-start.31
  311.5 323.9 %reduce-scatter.5.cloned.1.call-start = ((), (), s32[]{:S(2)}) async-start(), calls=%async_computation.8 | async-start | bytes 5013504 | tf_op jit(solution)/shard_map/reduce_scatter | solution.py:207
  372.2 3.9 copy-start.11
  372.2 3.9 copy-start.26
  376.1 3.6 copy-start.25
  406.2 2.0 copy-start.2
  406.2 2.0 copy-start.3
  406.2 2.0 copy-start.4
  406.2 2.1 copy-start.5
  406.2 2.2 copy-start.6
  406.2 2.3 copy-start.7
  408.8 0.9 copy-start.8
  425.2 1.1 copy-start.10
  425.2 1.2 copy-start.12
  425.2 427.5 %reduce-scatter.3.cloned.1.call-start = ((), (), s32[]{:S(2)}) async-start(), calls=%async_computation.5 | async-start | bytes 5013504 | tf_op jit(solution)/shard_map/reduce_scatter | solution.py:134
  429.9 205.5 %copy-start.1 = (bf16[48,3072]{1,0:T(8,128)(2,1)S(1)}, bf16[48,3072]{1,0:T(8,128)(2,1)}, u32[]{:S(2)}) copy-start(bf16[48,3072]{1,0:T(8,128)(2,1)} %param.9) | copy-start | bytes 884740
  429.9 205.5 %copy-start.21 = (f32[48]{0:T(128)S(1)}, f32[48]{0:T(128)}, u32[]{:S(2)}) copy-start(f32[48]{0:T(128)} %copy-done.20) | copy-start | bytes 580
  429.9 206.7 %copy-start.30 = (f32[48]{0:T(128)S(1)}, f32[48]{0:T(128)}, u32[]{:S(2)}) copy-start(f32[48]{0:T(128)} %copy-done.29) | copy-start | bytes 580
  429.9 206.7 %copy-start.24 = (f32[48]{0:T(128)S(1)}, f32[48]{0:T(128)}, u32[]{:S(2)}) copy-start(f32[48]{0:T(128)} %copy-done.23) | copy-start | bytes 580
  429.9 422.8 %copy-start.9 = (bf16[48,3072]{1,0:T(8,128)(2,1)S(1)}, bf16[48,3072]{1,0:T(8,128)(2,1)}, u32[]{:S(2)}) copy-start(bf16[48,3072]{1,0:T(8,128)(2,1)} %param.10) | copy-start | bytes 884740
  429.9 422.8 %copy-start.16 = (f32[1,1,3072]{2,0,1:T(1,128)S(1)}, f32[1,1,3072]{2,0,1:T(1,128)}, u32[]{:S(2)}) copy-start(f32[1,1,3072]{2,0,1:T(1,128)} %get-tuple-element.19) | copy-start | bytes 36868
Sparse Core Ops, SparseCore 0:
  14.5 102.7 all-gather.11
  123.9 38.9 all-gather.15
  164.8 38.6 all-gather.13
  205.9 99.9 all-gather.17
  308.1 39.1 all-gather.19
  348.9 38.4 all-gather.21
  425.3 210.0 reduce-scatter.4
  640.0 212.6 reduce-scatter.2
where the time goes:
time: 868 us; the launch traced here: 862 us
  waiting for transfers between devices  681 us (78%)
  matrix products  61.3 us (7%)
  blocking collectives  40.4 us (5%)
  between operations  39.6 us (5%)
  other arithmetic  22 us (3%)
  local copies, waits for them, and re-layouts  17.3 us (2%)
    reduce_scatter x1, waiting for transfers between devices, per_device(): lax.psum_scatter(jnp.dot(rows, w_out_flat, preferred_element_type=jnp.flo...  215 us
    reduce_scatter x1, waiting for transfers between devices, per_device(): lax.psum_scatter(lax.dot_general(rows, w_flat, (((1,), (1,)), ((), ())),...  205 us
    all_gather x1, waiting for transfers between devices, per_device(): lax.all_gather(modulated, 'head', axis=0, tiled=True)  102 us
    all_gather x1, waiting for transfers between devices, per_device(): lax.all_gather(cotangent, 'head', axis=0, tiled=True).astype(jnp.float32)  93 us
    all_gather x1, waiting for transfers between devices, per_device(): lax.all_gather(values, 'blk', axis=0, tiled=True)  38.5 us
    all_gather x1, waiting for transfers between devices, per_device(): lax.all_gather(keys, 'blk', axis=0, tiled=True)  22 us
    all_gather x1, blocking collectives, per_device(): lax.all_gather(total_all.astype(jnp.bfloat16), 'blk', axis=1, tiled=True)  21.2 us
    all_gather x1, blocking collectives, per_device(): lax.all_gather(delta_all.astype(jnp.bfloat16), 'blk', axis=1, tiled=True)  19.2 us
  transfers between devices with their start and end apart: 8, of which 7 were waited for; matrix products, arithmetic and copies ran while one was open for 5% of the time, Pallas kernels for 0%

commit v1 on v0

v1 whole, which is shorter than its diff:
```python
import functools

import jax
import jax.numpy as jnp
from jax import lax
from jax.experimental import pallas as pl
from jax.experimental.pallas import tpu as pltpu
from jax.sharding import PartitionSpec as P

EPS = 1e-6
TILE = 768
HD = 128
D = 3072
HALF = D // 2
SUB = 48
CH = 96
NZ = 8
F32 = jnp.float32
BF16 = jnp.bfloat16
FACTOR = HD ** -0.5
LOG2E = 1.4426950408889634
MESH = pl.DeviceIdType.MESH
NT = (((1,), (1,)), ((), ()))
TN = (((0,), (0,)), ((), ()))


def dot(a, b, dims=(((1,), (0,)), ((), ()))):
    return lax.dot_general(a, b, dims, preferred_element_type=F32)


def kernel(
    hid, cot, mods, wqkv, gains, wout, pairs, owner,
    res_out, gh_out,
    xs, cs, xg, cg, wq, wo, raw, psend, precv, dsend, drecv,
    qa, ka, va, doa, sta, attb, dqb, ot, dqt, dk, dv,
    rsnd, rrcv, rfin, ret,
    s_cross, r_cross, s_w, r_w, l_w, s_z, r_z, s_core, r_core,
    s_pl, r_pl, s_rs, r_rs, s_ret, r_ret,
):
    head, blk = lax.axis_index("head"), lax.axis_index("blk")
    yh, z = head // 8, lax.rem(head, 8)
    x, yl, c = blk // 4, lax.rem(blk // 2, 2), lax.rem(blk, 2)
    y = yh * 2 + yl

    def dev(yh=yh, z=z, x=x, yl=yl, c=c):
        return (yh * 8 + z, (x * 2 + yl) * 2 + c)

    def at_y(yy):
        yy = lax.rem(yy + 4, 4)
        return dev(yh=yy // 2, yl=lax.rem(yy, 2))

    def at_x(xx):
        return dev(x=lax.rem(xx + 4, 4))

    def at_z(zz):
        return dev(z=lax.rem(zz + 8, 8))

    sibling = dev(c=1 - c)
    wpartner = dev(yh=1 - yh, yl=1 - yl)
    own = c == yh

    barrier = pltpu.get_barrier_semaphore()
    partners = [
        at_x(x + 1), at_x(x - 1), at_y(y + 1), at_y(y - 1), at_z(z + 1), at_z(z - 1),
        sibling, dev(yh=1 - yh), dev(yh=1 - yh, c=1 - c),
    ]
    for p in partners:
        pl.semaphore_signal(barrier, inc=1, device_id=p, device_id_type=MESH)

    shift = mods[0:1, :]
    scale = mods[1:2, :]
    gate = mods[2:3, :]

    def normed():
        rows = hid[...].astype(F32)
        center = rows - jnp.mean(rows, axis=-1, keepdims=True)
        spread = jnp.mean(center * center, axis=-1, keepdims=True)
        r = lax.rsqrt(spread + EPS)
        return center * r, r

    hat, _ = normed()
    xs[...] = (hat * (1.0 + scale) + shift).astype(BF16)
    cs[...] = (cot[...].astype(F32) * gate).astype(BF16)

    pl.semaphore_wait(barrier, len(partners))

    def remote(src, dst, ss, rs, target):
        return pltpu.make_async_remote_copy(
            src_ref=src, dst_ref=dst, send_sem=ss, recv_sem=rs,
            device_id=target, device_id_type=MESH,
        )

    pending = []

    def send(src, dst, ss, rs, target):
        copy = remote(src, dst, ss, rs, target)
        copy.start()
        pending.append(copy.wait_send)

    def arrived(dst, rs):
        remote(dst, dst, rs, rs, sibling).wait_recv()

    def rows_of(zz, sub, count=SUB):
        return pl.ds(pl.multiple_of(zz * CH + sub * SUB, 16), count)

    def cross_send(n, stage, grid):
        for h in range(2):
            src = stage.at[:, h * HALF:(h + 1) * HALF]
            dst = grid.at[rows_of(z, yh)]
            here = jnp.logical_and(own, c == h)

            @pl.when(here)
            def _():
                pltpu.make_async_copy(src, dst, r_cross.at[n, yh]).start()

            copy = remote(src, dst, s_cross.at[n, h], r_cross.at[n, yh], dev(yh=c, c=h))

            @pl.when(jnp.logical_not(here))
            def _():
                copy.start()

            def done(here=here, copy=copy):
                @pl.when(jnp.logical_not(here))
                def _():
                    copy.wait_send()
            pending.append(done)

    def cross_wait(n, grid):
        for sub in range(2):
            dst = grid.at[rows_of(z, sub)]
            pltpu.make_async_copy(dst, dst, r_cross.at[n, sub]).wait()

    cross_send(0, xs, xg)
    wq_src = wqkv.at[pl.ds(pl.multiple_of(c * HALF, 16), HALF)]
    wq_dst = wq.at[:, pl.ds(pl.multiple_of(yh * 384, 128), 384)]
    wo_src = wout.at[:, pl.ds(pl.multiple_of(c * HALF, 128), HALF)]
    wo_dst = wo.at[pl.ds(pl.multiple_of(yh * HD, 16), HD)]
    send(wq_src, wq_dst, s_w.at[0], r_w.at[0], wpartner)
    wq_local = pltpu.make_async_copy(wq_src, wq_dst, l_w.at[0])
    wq_local.start()
    wo_local = pltpu.make_async_copy(wo_src, wo_dst, l_w.at[1])
    wo_local.start()
    cross_send(1, cs, cg)
    send(wo_src, wo_dst, s_w.at[1], r_w.at[1], wpartner)

    def z_piece(j, sign, off):
        chunk = lax.rem(z + off + 16, 8)
        if j < 4:
            return rows_of(chunk, 0, CH)
        return rows_of(chunk, 0 if sign > 0 else 1)

    def z_start(n, grid, j):
        for i, sign in enumerate((1, -1)):
            ref = grid.at[z_piece(j, sign, -sign * (j - 1))]
            k = (j - 1) * 2 + i
            send(ref, ref, s_z.at[n, k], r_z.at[n, k], at_z(z + sign))

    def z_wait(n, grid, j):
        for i, sign in enumerate((1, -1)):
            arrived(grid.at[z_piece(j, sign, -sign * j)], r_z.at[n, (j - 1) * 2 + i])

    cross_wait(0, xg)
    z_start(0, xg, 1)
    z_wait(0, xg, 1)
    z_start(0, xg, 2)
    z_wait(0, xg, 2)
    z_start(0, xg, 3)
    z_wait(0, xg, 3)
    z_start(0, xg, 4)
    cross_wait(1, cg)
    z_start(1, cg, 1)
    z_wait(0, xg, 4)
    wq_local.wait()
    arrived(wq.at[:, pl.ds(pl.multiple_of((1 - yh) * 384, 128), 384)], r_w.at[0])

    def pick(first, second):
        return jnp.where(c == 0, first, second), jnp.where(c == 0, second, first)

    def qkv_rows(t, carry):
        r = pl.ds(pl.multiple_of(t * 256, 256), 256)
        part = dot(xg[r, :], wq[...])
        mine, other = pick(part[:, :384], part[:, 384:])
        raw[r, :] = mine
        psend[r, :] = other
        remote(psend.at[r], precv.at[r], s_core.at[t], r_core.at[t], sibling).start()
        return carry

    lax.fori_loop(0, 3, qkv_rows, 0)

    slot = x * 4 + y

    def rms(source, row):
        return lax.rsqrt(jnp.mean(source * source, axis=-1, keepdims=True) + EPS) * gains[row:row + 1, :]

    def norm_rows(t, carry):
        r = pl.ds(pl.multiple_of(t * 256, 256), 256)
        arrived(precv.at[r], r_core.at[t])
        total = raw[r, :] + precv[r, :]
        raw[r, :] = total
        query, key = total[:, :HD], total[:, HD:2 * HD]
        qa[slot, r, :] = (query * rms(query, 0)).astype(BF16)
        ka[slot, r, :] = (key * rms(key, 1)).astype(BF16)
        va[slot, r, :] = total[:, 2 * HD:].astype(BF16)
        return carry

    lax.fori_loop(0, 3, norm_rows, 0)

    def plane(n, ref, rows, swap):
        half = rows // 2

        def place(oa, ob):
            ox, oy = (ob, oa) if swap else (oa, ob)
            return lax.rem(x + ox + 4, 4) * 4 + lax.rem(y + oy + 4, 4)

        def target(axis, sign):
            on_x = (axis == 0) != swap
            return at_x(x + sign) if on_x else at_y(y + sign)

        moves = [(0, 1, 0, 0, None), (0, -1, 0, 0, None), (0, 1, -1, 0, 0), (0, -1, 1, 0, 1)]
        for oa in (0, -1, 1, -2):
            moves += [(1, 1, oa, 0, None), (1, -1, oa, 0, None), (1, 1, oa, -1, 0), (1, -1, oa, 1, 1)]

        def view(oa, ob, part):
            s = place(oa, ob)
            if part is None:
                return ref.at[s]
            return ref.at[s, pl.ds(part * half, half)]

        def start(*ids):
            for i in ids:
                axis, sign, oa, ob, part = moves[i]
                src = view(oa, ob, part)
                send(src, src, s_pl.at[n, i], r_pl.at[n, i], target(axis, sign))

        def wait(*ids):
            for i in ids:
                axis, sign, oa, ob, part = moves[i]
                if axis == 0:
                    oa = oa - sign
                else:
                    ob = ob - sign
                arrived(view(oa, ob, part), r_pl.at[n, i])

        def round_(k):
            if k == 1:
                start(0, 1, 4, 5)
            elif k == 2:
                wait(0, 1)
                start(2, 3, 8, 9, 12, 13)
                wait(4, 5)
                start(6, 7)
            elif k == 3:
                wait(2, 3)
                start(16, 17)
                wait(8, 9, 12, 13)
                start(10, 11, 14, 15)
            elif k == 4:
                wait(16, 17)
                start(18, 19)
            else:
                wait(6, 7, 10, 11, 14, 15, 18, 19)
        return round_

    k_round = plane(0, ka, TILE, False)
    v_round = plane(1, va, TILE, True)
    q_round = plane(2, qa, TILE, False)
    o_round = plane(3, doa, TILE, True)
    s_round = plane(4, sta, 16, False)

    k_round(1)
    v_round(1)
    z_wait(1, cg, 1)
    z_start(1, cg, 2)
    k_round(2)
    v_round(2)
    z_wait(1, cg, 2)
    z_start(1, cg, 3)
    k_round(3)
    v_round(3)
    z_wait(1, cg, 3)
    z_start(1, cg, 4)
    k_round(4)
    v_round(4)
    q_round(1)
    z_wait(1, cg, 4)
    wo_local.wait()
    arrived(wo.at[pl.ds(pl.multiple_of((1 - yh) * HD, 16), HD)], r_w.at[1])

    def grad_rows(t, carry):
        r = pl.ds(pl.multiple_of(t * 256, 256), 256)
        part = dot(cg[r, :], wo[...], NT)
        mine, other = pick(part[:, :HD], part[:, HD:])
        drecv[0, r, :] = mine
        dsend[r, :] = other
        return carry

    lax.fori_loop(0, 3, grad_rows, 0)
    send(dsend, drecv.at[1], s_core.at[3], r_core.at[3], sibling)
    k_round(5)
    v_round(5)
    arrived(drecv.at[1], r_core.at[3])
    doa[slot] = (drecv[0] + drecv[1]).astype(BF16)
    o_round(1)

    def position(s):
        return (s // 4 * 2 + s % 2) * 2 + (s % 4) // 2

    tile = owner[(x * 2 + yl) * 2 + yh]
    before = lax.rem(tile + 15, 16)
    after = lax.rem(tile + 1, 16)
    slot_b = jnp.int32(0)
    slot_a = jnp.int32(0)
    for s in range(16):
        o = owner[position(s)]
        slot_b = jnp.where(o == before, s, slot_b)
        slot_a = jnp.where(o == after, s, slot_a)

    def lists(a, b):
        hit = jnp.float32(0.0)
        for n in range(3):
            hit = jnp.where(pairs[a, n] == b, 1.0, hit)
        return hit

    one = jnp.float32(1.0)
    key_tiles = [(slot, one), (slot_b, lists(tile, before)), (slot_a, lists(tile, after))]
    query_tiles = [(slot_b, lists(before, tile)), (slot_a, lists(after, tile))]
    EXPC = FACTOR * LOG2E

    def scores(keys_, query_):
        return dot(keys_, query_, NT) * EXPC

    ot[...] = jnp.zeros_like(ot)
    total = jnp.zeros((1, TILE), F32)

    def attend(total, entry):
        s, valid = entry

        def block(t, total):
            r = pl.ds(pl.multiple_of(t * 256, 256), 256)
            e = jnp.exp2(scores(ka[s, r, :], qa[slot])) * valid
            ot[...] += dot(va[s, r, :], e.astype(BF16), TN)
            return total + jnp.sum(e, axis=0, keepdims=True)
        return lax.fori_loop(0, 3, block, total)

    total = attend(total, key_tiles[0])
    q_round(2)
    o_round(2)
    total = attend(total, key_tiles[1])
    q_round(3)
    o_round(3)
    total = attend(total, key_tiles[2])
    q_round(4)
    o_round(4)
    out_t = (ot[...] / total).astype(BF16).astype(F32)
    attb[c] = out_t.T.astype(BF16)
    send(attb.at[c], attb.at[c], s_core.at[4], r_core.at[4], sibling)
    lse = jnp.log2(total)
    delta = jnp.sum(out_t * doa[slot].astype(F32).T, axis=0, keepdims=True)
    for i in range(6):
        sta[slot, i:i + 1, :] = lse[:, i * HD:(i + 1) * HD]
        sta[slot, 8 + i:9 + i, :] = delta[:, i * HD:(i + 1) * HD]
    s_round(1)

    base = {4: 0, 3: SUB, 2: SUB + CH, 1: SUB + 2 * CH}

    def rs_step(n, partial, j):
        for i, sign in enumerate((1, -1)):
            dest = lax.rem(z + sign * j + 8, 8)
            k = (j - 1) * 2 + i
            if j == 4:
                value = partial(rows_of(dest, i))
                r = pl.ds(0, SUB)
            else:
                value = partial(rows_of(dest, 0, CH))
                r = pl.ds(base[j], CH)
                prev = pl.ds(base[j + 1], SUB if j == 3 else CH)
                arrived(rrcv.at[n, i, prev], r_rs.at[n, k + 2])
                got = rrcv[n, i, prev, :].astype(F32)
                if j == 3:
                    zero = jnp.zeros_like(got)
                    got = jnp.concatenate([got, zero] if i == 0 else [zero, got], axis=0)
                value = value + got
            rsnd[n, i, r, :] = value.astype(BF16)
            send(rsnd.at[n, i, r], rrcv.at[n, i, r], s_rs.at[n, k], r_rs.at[n, k], at_z(z + sign))

    def rs_finish(n, partial):
        value = partial(rows_of(z, 0, CH))
        r = pl.ds(base[1], CH)
        for i in range(2):
            arrived(rrcv.at[n, i, r], r_rs.at[n, i])
            value = value + rrcv[n, i, r, :].astype(F32)
        rfin[n] = value.astype(BF16)
        cols = pl.ds(pl.multiple_of(c * HALF, 128), HALF)
        for sub in range(2):
            src = rfin.at[n, pl.ds(sub * SUB, SUB)]
            dst = ret.at[n, :, cols]
            here = jnp.logical_and(own, yh == sub)

            @pl.when(here)
            def _():
                pltpu.make_async_copy(src, dst, r_ret.at[n, c]).start()

            copy = remote(src, dst, s_ret.at[n, sub], r_ret.at[n, c], dev(yh=sub, c=yh))

            @pl.when(jnp.logical_not(here))
            def _():
                copy.start()

            def done(here=here, copy=copy):
                @pl.when(jnp.logical_not(here))
                def _():
                    copy.wait_send()
            pending.append(done)

    def ret_wait(n):
        for h in range(2):
            dst = ret.at[n, :, h * HALF:(h + 1) * HALF]
            pltpu.make_async_copy(dst, dst, r_ret.at[n, h]).wait()

    def proj_part(r):
        both = jnp.concatenate([attb[0, r, :], attb[1, r, :]], axis=1)
        return dot(both, wo[...])

    def dmod_part(r):
        both = jnp.concatenate([dqb[0, r, :], dqb[1, r, :]], axis=1)
        return dot(both, wq[...], NT)

    def backward(key_slot, query_slot, valid, lse, delta, to_query, to_key, first=False):
        def block(t, carry):
            r = pl.ds(pl.multiple_of(t * 256, 256), 256)
            keys_ = ka[key_slot, r, :]
            query_ = qa[query_slot]
            grad_ = doa[query_slot]
            p = jnp.exp2(scores(keys_, query_) - lse) * valid
            d_prob = dot(va[key_slot, r, :], grad_, NT)
            ds = (p * (d_prob - delta)).astype(BF16)
            if to_query:
                dqt[...] += dot(keys_, ds, TN)
            if to_key:
                new_v = dot(p.astype(BF16), grad_)
                new_k = dot(ds, query_)
                if first:
                    dv[r, :] = new_v
                    dk[r, :] = new_k
                else:
                    dv[r, :] += new_v
                    dk[r, :] += new_k
            return carry
        lax.fori_loop(0, 3, block, 0)

    dqt[...] = jnp.zeros_like(dqt)
    arrived(attb.at[1 - c], r_core.at[4])
    rs_step(0, proj_part, 4)
    backward(slot, slot, one, lse, delta, True, True, True)
    rs_step(0, proj_part, 3)
    s_round(2)
    backward(slot_b, slot, key_tiles[1][1], lse, delta, True, False)
    rs_step(0, proj_part, 2)
    s_round(3)
    backward(slot_a, slot, key_tiles[2][1], lse, delta, True, False)
    rs_step(0, proj_part, 1)
    s_round(4)
    q_round(5)
    o_round(5)
    s_round(5)

    def from_stats(s, first):
        return jnp.concatenate([sta[s, first + i:first + i + 1, :] for i in range(6)], axis=1)

    s, valid = query_tiles[0]
    backward(slot, s, valid, from_stats(s, 0), from_stats(s, 8), False, True)
    rs_finish(0, proj_part)
    s, valid = query_tiles[1]
    backward(slot, s, valid, from_stats(s, 0), from_stats(s, 8), False, True)

    def through_norm(source, grad, row):
        r = lax.rsqrt(jnp.mean(source * source, axis=-1, keepdims=True) + EPS)
        g = grad * gains[row:row + 1, :]
        return r * g - source * (r * r * r) * jnp.mean(source * g, axis=-1, keepdims=True)

    dqt_rows = drecv
    dqt_rows[0] = dqt[...].T * FACTOR

    def norm_back(t, carry):
        r = pl.ds(pl.multiple_of(t * 256, 256), 256)
        rows = raw[r, :]
        dqb[c, r, :HD] = through_norm(rows[:, :HD], dqt_rows[0, r, :], 0).astype(BF16)
        dqb[c, r, HD:2 * HD] = through_norm(rows[:, HD:2 * HD], dk[r, :] * FACTOR, 1).astype(BF16)
        dqb[c, r, 2 * HD:] = dv[r, :].astype(BF16)
        return carry

    lax.fori_loop(0, 3, norm_back, 0)
    send(dqb.at[c], dqb.at[c], s_core.at[5], r_core.at[5], sibling)
    arrived(dqb.at[1 - c], r_core.at[5])
    rs_step(1, dmod_part, 4)
    rs_step(1, dmod_part, 3)
    rs_step(1, dmod_part, 2)
    rs_step(1, dmod_part, 1)

    ret_wait(0)
    res_out[...] = (hid[...].astype(F32) + gate * ret[0].astype(F32)).astype(BF16)
    rs_finish(1, dmod_part)
    hat, r = normed()
    ret_wait(1)
    g = ret[1].astype(F32) * (1.0 + scale)
    d_in = r * (g - jnp.mean(g, axis=-1, keepdims=True) - hat * jnp.mean(g * hat, axis=-1, keepdims=True))
    gh_out[...] = (cot[...].astype(F32) + d_in).astype(BF16)

    for done in pending:
        done()
    for t in range(3):
        r = pl.ds(t * 256, 256)
        remote(psend.at[r], precv.at[r], s_core.at[t], r_core.at[t], sibling).wait_send()


def per_device(hidden, cotangent, step_index, mod_table, w_qkv, qk_gains, w_out, tile_pairs, tile_owner):
    vm = pl.BlockSpec(memory_space=pltpu.VMEM)
    sm = pl.BlockSpec(memory_space=pltpu.SMEM)
    hbm = pl.BlockSpec(memory_space=pl.ANY)
    dma = pltpu.SemaphoreType.DMA
    mods = lax.dynamic_index_in_dim(mod_table, step_index[0], 0, keepdims=False)
    V = pltpu.VMEM
    return pl.pallas_call(
        kernel,
        out_shape=[jax.ShapeDtypeStruct(hidden.shape, BF16)] * 2,
        in_specs=[vm, vm, vm, hbm, vm, hbm, sm, sm],
        out_specs=[vm, vm],
        scratch_shapes=[
            V((SUB, D), BF16), V((SUB, D), BF16), V((TILE, HALF), BF16), V((TILE, HALF), BF16),
            V((HALF, 768), BF16), V((256, HALF), BF16), V((TILE, 384), F32), V((TILE, 384), F32), V((TILE, 384), F32),
            V((TILE, HD), F32), V((2, TILE, HD), F32),
            V((16, TILE, HD), BF16), V((16, TILE, HD), BF16), V((16, TILE, HD), BF16), V((16, TILE, HD), BF16),
            V((16, 16, HD), F32), V((2, TILE, HD), BF16), V((2, TILE, 384), BF16),
            V((HD, TILE), F32), V((HD, TILE), F32), V((TILE, HD), F32), V((TILE, HD), F32),
            V((2, 2, 336, HALF), BF16), V((2, 2, 336, HALF), BF16), V((2, CH, HALF), BF16), V((2, SUB, D), BF16),
            dma((2, 2)), dma((2, 2)), dma((2,)), dma((2,)), dma((2,)), dma((2, 8)), dma((2, 8)), dma((6,)), dma((6,)),
            dma((5, 20)), dma((5, 20)), dma((2, 8)), dma((2, 8)), dma((2, 2)), dma((2, 2)),
        ],
        compiler_params=pltpu.CompilerParams(
            collective_id=0, has_side_effects=True, vmem_limit_bytes=60 * 2 ** 20
        ),
        name="sublayer",
    )(
        hidden, cotangent, mods, w_qkv.reshape(D, 384),
        qk_gains, w_out.reshape(HD, D), tile_pairs, tile_owner,
    )


def solution(mesh):
    rows = P(("blk", "head"), None)
    in_specs = (
        rows, rows, P(), P(), P(None, "head", None), P(), P("head", None, None), P(), P(),
    )
    return jax.shard_map(
        per_device, mesh=mesh, in_specs=in_specs, out_specs=(rows, rows), check_vma=False
    )
```

time: 868 us -> 199 us (0.23)
  waiting for transfers between devices: 681 us -> 0 us
  Pallas kernels: 0 us -> 192 us
  matrix products: 61.3 us -> 0 us
  blocking collectives: 40.4 us -> 0 us
  between operations: 39.6 us -> 1.4 us
  other arithmetic: 22 us -> 0 us
  local copies, waits for them, and re-layouts: 17.3 us -> 5.42 us
    reduce_scatter x2 -> x0, waiting for transfers between devices: 420 us -> none  [the longest x1 215 us: per_device(): lax.psum_scatter(jnp.dot(rows, w_out_flat, preferred_element_type=jnp.flo...]
    all_gather x6 -> x0, waiting for transfers between devices: 259 us -> none  [the longest x1 102 us: per_device(): lax.all_gather(modulated, 'head', axis=0, tiled=True)]
    pallas_call x0 -> x1, Pallas kernels: none -> 192 us  [per_device(): pl.pallas_call(kernel, out_shape=[jax.ShapeDtypeStruct(hidden.shape, BF16...]
    dot_general x16 -> x0, matrix products: 61.3 us -> none  [the longest x3 11.1 us: score_terms(): jnp.einsum('qhd,khd->hqk', query, keys, preferred_element_type=jnp.float32)]
    all_gather x2 -> x0, blocking collectives: 40.4 us -> none  [the longest x1 21.2 us: per_device(): lax.all_gather(total_all.astype(jnp.bfloat16), 'blk', axis=1, tiled=True)]
  transfers between devices with their start and end apart: 8 -> 0, of which waited for: 7 -> 0; matrix products, arithmetic and copies ran while one was open for 5% -> 0% of each run, Pallas kernels for 0% -> 0%
where the time goes in v1:
time: 199 us
  Pallas kernels  192 us (96%)
  local copies, waits for them, and re-layouts  5.42 us (3%)
    pallas_call x1, Pallas kernels, per_device(): pl.pallas_call(kernel, out_shape=[jax.ShapeDtypeStruct(hidden.shape, BF16...  192 us
    unnamed x6, local copies, waits for them, and re-layouts  5.39 us

profile of v1, /device:TPU:9, one launch (start us, length us, event | category | flops | bytes accessed | tf_op | source)
XLA Modules:
  0.0 198.8 jit_solution(13298488198057293344)
XLA Ops:
  0.6 0.0 copy-start
  1.4 1.4 copy.12.pairs
  2.7 0.0 copy-done
  2.8 0.6 copy.15
  3.4 192.0 %sublayer.1 = (bf16[48,3072]{1,0:T(8,128)(2,1)}, bf16[48,3072]{1,0:T(8,128)(2,1)}) custom-call(bf16[48,3072]{1,0:T(8,128)(2,1)} %hid.1, bf16[48,3072]{1,0:T(8,128)(2,1)} %cot.1, f32[3,3072]{1,0:T(4,128)} %bitcast.11, bf16[3072,384]{1,0:T(8,128)(2,1)} %bitcast.9, f32[2,128]{1,0:T(2,128)} %gains.1, bf16[128,3072]{1,0:T(8,128)(2,1)} %bitcast.10, ...), custom_call_target="tpu_custom_call" | custom-call | tf_op jit(solution)/shard_map/sublayer/pallas_call | solution.py:523
  195.4 1.7 copy.19
  197.1 1.7 copy.20
  (1 shorter events, 0.0 us)
Async XLA Ops:
  0.6 2.1 %copy-start = (f32[32,3,3072]{2,0,1:T(8,128)S(1)}, f32[32,3,3072]{2,0,1:T(8,128)}, u32[]{:S(2)}) copy-start(f32[32,3,3072]{2,0,1:T(8,128)} %param.12) | copy-start | bytes 3538948

commit v2 on v1

--- a/solution.py
+++ b/solution.py
@@ -33,7 +33,7 @@
     res_out, gh_out,
     xs, cs, xg, cg, wq, wo, raw, psend, precv, dsend, drecv,
     qa, ka, va, doa, sta, attb, dqb, ot, dqt, dk, dv,
-    rsnd, rrcv, rfin, ret,
+    rsnd, rrcv, rfin, ret, pbuf,
     s_cross, r_cross, s_w, r_w, l_w, s_z, r_z, s_core, r_core,
     s_pl, r_pl, s_rs, r_rs, s_ret, r_ret,
 ):
@@ -131,47 +131,79 @@
             pltpu.make_async_copy(dst, dst, r_cross.at[n, sub]).wait()
 
     cross_send(0, xs, xg)
-    wq_src = wqkv.at[pl.ds(pl.multiple_of(c * HALF, 16), HALF)]
-    wq_dst = wq.at[:, pl.ds(pl.multiple_of(yh * 384, 128), 384)]
-    wo_src = wout.at[:, pl.ds(pl.multiple_of(c * HALF, 128), HALF)]
-    wo_dst = wo.at[pl.ds(pl.multiple_of(yh * HD, 16), HD)]
-    send(wq_src, wq_dst, s_w.at[0], r_w.at[0], wpartner)
-    wq_local = pltpu.make_async_copy(wq_src, wq_dst, l_w.at[0])
+    def lanes(first, size):
+        return pl.ds(pl.multiple_of(first, 128), size)
+
+    def rows16(first, size):
+        return pl.ds(pl.multiple_of(first, 16), size)
+
+    def w_view(n, hh, ox, part=None):
+        q = lax.rem(x + ox + 4, 4) * 384
+        if n == 0:
+            size = 384 if part is None else 192
+            return wq.at[rows16(q + (part or 0) * 192, size), lanes(hh * 384, 384)]
+        size = HD if part is None else HD // 2
+        return wo.at[rows16(hh * HD + (part or 0) * 64, size), lanes(q, 384)]
+
+    w_moves = [(1, 0, None), (-1, 0, None), (1, -1, 0), (-1, 1, 1)]
+
+    def w_start(n, *ids):
+        for i in ids:
+            sign, ox, part = w_moves[i]
+            ref = w_view(n, 1 - yh, ox, part)
+            send(ref, ref, s_w.at[n, i], r_w.at[n, i], at_x(x + sign))
+
+    def w_wait(n, *ids):
+        for i in ids:
+            sign, ox, part = w_moves[i]
+            arrived(w_view(n, 1 - yh, ox - sign, part), r_w.at[n, i])
+
+    def w_quarter(n):
+        arrived(w_view(n, 1 - yh, 0), r_w.at[n, 4])
+
+    send(wqkv.at[rows16(c * HALF + x * 384, 384)], w_view(0, yh, 0), s_w.at[0, 4], r_w.at[0, 4], wpartner)
+    wq_local = pltpu.make_async_copy(wqkv.at[rows16(c * HALF, HALF)], wq.at[:, lanes(yh * 384, 384)], l_w.at[0])
+    wo_local = pltpu.make_async_copy(wout.at[:, lanes(c * HALF, HALF)], wo.at[rows16(yh * HD, HD)], l_w.at[1])
     wq_local.start()
-    wo_local = pltpu.make_async_copy(wo_src, wo_dst, l_w.at[1])
     wo_local.start()
     cross_send(1, cs, cg)
-    send(wo_src, wo_dst, s_w.at[1], r_w.at[1], wpartner)
-
-    def z_piece(j, sign, off):
-        chunk = lax.rem(z + off + 16, 8)
-        if j < 4:
-            return rows_of(chunk, 0, CH)
-        return rows_of(chunk, 0 if sign > 0 else 1)
-
-    def z_start(n, grid, j):
+    send(wout.at[:, lanes(c * HALF + x * 384, 384)], w_view(1, yh, 0), s_w.at[1, 4], r_w.at[1, 4], wpartner)
+
+    def z_piece(grid, off, h):
+        return grid.at[rows_of(lax.rem(z + off + 16, 8), h)]
+
+    def z_step(n, grid, j):
+        for h in range(2):
+            for i, sign in enumerate((1, -1)):
+                if j > 1:
+                    arrived(z_piece(grid, -sign * (j - 1), h), r_z.at[n, (j - 2) * 4 + i * 2 + h])
+                if j < 4 or h == i:
+                    ref = z_piece(grid, -sign * (j - 1), h)
+                    k = (j - 1) * 4 + i * 2 + h
+                    send(ref, ref, s_z.at[n, k], r_z.at[n, k], at_z(z + sign))
+
+    def z_end(n, grid):
         for i, sign in enumerate((1, -1)):
-            ref = grid.at[z_piece(j, sign, -sign * (j - 1))]
-            k = (j - 1) * 2 + i
-            send(ref, ref, s_z.at[n, k], r_z.at[n, k], at_z(z + sign))
-
-    def z_wait(n, grid, j):
-        for i, sign in enumerate((1, -1)):
-            arrived(grid.at[z_piece(j, sign, -sign * j)], r_z.at[n, (j - 1) * 2 + i])
+            arrived(z_piece(grid, -sign * 4, i), r_z.at[n, 12 + i * 3])
 
     cross_wait(0, xg)
-    z_start(0, xg, 1)
-    z_wait(0, xg, 1)
-    z_start(0, xg, 2)
-    z_wait(0, xg, 2)
-    z_start(0, xg, 3)
-    z_wait(0, xg, 3)
-    z_start(0, xg, 4)
+    z_step(0, xg, 1)
+    w_quarter(0)
+    w_start(0, 0, 1)
+    z_step(0, xg, 2)
     cross_wait(1, cg)
-    z_start(1, cg, 1)
-    z_wait(0, xg, 4)
+    w_quarter(1)
+    w_start(1, 0, 1)
+    z_step(0, xg, 3)
+    w_wait(0, 0, 1)
+    w_start(0, 2, 3)
+    w_wait(1, 0, 1)
+    w_start(1, 2, 3)
+    z_step(0, xg, 4)
+    z_step(1, cg, 1)
+    w_wait(0, 2, 3)
     wq_local.wait()
-    arrived(wq.at[:, pl.ds(pl.multiple_of((1 - yh) * 384, 128), 384)], r_w.at[0])
+    z_end(0, xg)
 
     def pick(first, second):
         return jnp.where(c == 0, first, second), jnp.where(c == 0, second, first)
@@ -269,22 +301,14 @@
 
     k_round(1)
     v_round(1)
-    z_wait(1, cg, 1)
-    z_start(1, cg, 2)
+    z_step(1, cg, 2)
     k_round(2)
     v_round(2)
-    z_wait(1, cg, 2)
-    z_start(1, cg, 3)
-    k_round(3)
-    v_round(3)
-    z_wait(1, cg, 3)
-    z_start(1, cg, 4)
-    k_round(4)
-    v_round(4)
-    q_round(1)
-    z_wait(1, cg, 4)
+    z_step(1, cg, 3)
+    z_step(1, cg, 4)
+    w_wait(1, 2, 3)
     wo_local.wait()
-    arrived(wo.at[pl.ds(pl.multiple_of((1 - yh) * HD, 16), HD)], r_w.at[1])
+    z_end(1, cg)
 
     def grad_rows(t, carry):
         r = pl.ds(pl.multiple_of(t * 256, 256), 256)
@@ -296,11 +320,10 @@
 
     lax.fori_loop(0, 3, grad_rows, 0)
     send(dsend, drecv.at[1], s_core.at[3], r_core.at[3], sibling)
-    k_round(5)
-    v_round(5)
+    k_round(3)
+    v_round(3)
     arrived(drecv.at[1], r_core.at[3])
     doa[slot] = (drecv[0] + drecv[1]).astype(BF16)
-    o_round(1)
 
     def position(s):
         return (s // 4 * 2 + s % 2) * 2 + (s % 4) // 2
@@ -343,14 +366,14 @@
         return lax.fori_loop(0, 3, block, total)
 
     total = attend(total, key_tiles[0])
-    q_round(2)
-    o_round(2)
+    k_round(4)
+    v_round(4)
+    q_round(1)
+    o_round(1)
+    k_round(5)
+    v_round(5)
     total = attend(total, key_tiles[1])
-    q_round(3)
-    o_round(3)
     total = attend(total, key_tiles[2])
-    q_round(4)
-    o_round(4)
     out_t = (ot[...] / total).astype(BF16).astype(F32)
     attb[c] = out_t.T.astype(BF16)
     send(attb.at[c], attb.at[c], s_core.at[4], r_core.at[4], sibling)
@@ -364,32 +387,34 @@
     base = {4: 0, 3: SUB, 2: SUB + CH, 1: SUB + 2 * CH}
 
     def rs_step(n, partial, j):
-        for i, sign in enumerate((1, -1)):
-            dest = lax.rem(z + sign * j + 8, 8)
-            k = (j - 1) * 2 + i
-            if j == 4:
-                value = partial(rows_of(dest, i))
-                r = pl.ds(0, SUB)
-            else:
-                value = partial(rows_of(dest, 0, CH))
-                r = pl.ds(base[j], CH)
-                prev = pl.ds(base[j + 1], SUB if j == 3 else CH)
-                arrived(rrcv.at[n, i, prev], r_rs.at[n, k + 2])
-                got = rrcv[n, i, prev, :].astype(F32)
-                if j == 3:
-                    zero = jnp.zeros_like(got)
-                    got = jnp.concatenate([got, zero] if i == 0 else [zero, got], axis=0)
-                value = value + got
-            rsnd[n, i, r, :] = value.astype(BF16)
-            send(rsnd.at[n, i, r], rrcv.at[n, i, r], s_rs.at[n, k], r_rs.at[n, k], at_z(z + sign))
+        if j == 4:
+            pbuf[:CH, :] = partial([rows_of(lax.rem(z + 4, 8), 0, CH)])
+        else:
+            pbuf[...] = partial([rows_of(lax.rem(z + sign * j + 8, 8), 0, CH) for sign in (1, -1)])
+        for h in range(2):
+            for i, sign in enumerate((1, -1)):
+                if j == 4 and h != i:
+                    continue
+                first = h * SUB + (0 if j == 4 else i * CH)
+                value = pbuf[first:first + SUB, :]
+                r = pl.ds(0 if j == 4 else base[j] + h * SUB, SUB)
+                k = (j - 1) * 4 + i * 2 + h
+                if j < 3 or (j == 3 and h == i):
+                    prev = pl.ds(0 if j == 3 else base[j + 1] + h * SUB, SUB)
+                    arrived(rrcv.at[n, i, prev], r_rs.at[n, k + 4])
+                    value = value + rrcv[n, i, prev, :].astype(F32)
+                rsnd[n, i, r, :] = value.astype(BF16)
+                send(rsnd.at[n, i, r], rrcv.at[n, i, r], s_rs.at[n, k], r_rs.at[n, k], at_z(z + sign))
 
     def rs_finish(n, partial):
-        value = partial(rows_of(z, 0, CH))
-        r = pl.ds(base[1], CH)
-        for i in range(2):
-            arrived(rrcv.at[n, i, r], r_rs.at[n, i])
-            value = value + rrcv[n, i, r, :].astype(F32)
-        rfin[n] = value.astype(BF16)
+        pbuf[:CH, :] = partial([rows_of(z, 0, CH)])
+        for h in range(2):
+            value = pbuf[h * SUB:(h + 1) * SUB, :]
+            r = pl.ds(base[1] + h * SUB, SUB)
+            for i in range(2):
+                arrived(rrcv.at[n, i, r], r_rs.at[n, i * 2 + h])
+                value = value + rrcv[n, i, r, :].astype(F32)
+            rfin[n, h * SUB:(h + 1) * SUB, :] = value.astype(BF16)
         cols = pl.ds(pl.multiple_of(c * HALF, 128), HALF)
         for sub in range(2):
             src = rfin.at[n, pl.ds(sub * SUB, SUB)]
@@ -417,13 +442,16 @@
             dst = ret.at[n, :, h * HALF:(h + 1) * HALF]
             pltpu.make_async_copy(dst, dst, r_ret.at[n, h]).wait()
 
-    def proj_part(r):
-        both = jnp.concatenate([attb[0, r, :], attb[1, r, :]], axis=1)
-        return dot(both, wo[...])
-
-    def dmod_part(r):
-        both = jnp.concatenate([dqb[0, r, :], dqb[1, r, :]], axis=1)
-        return dot(both, wq[...], NT)
+    def stack(ref, spans):
+        return jnp.concatenate(
+            [jnp.concatenate([ref[0, r, :], ref[1, r, :]], axis=1) for r in spans], axis=0
+        )
+
+    def proj_part(spans):
+        return dot(stack(attb, spans), wo[...])
+
+    def dmod_part(spans):
+        return dot(stack(dqb, spans), wq[...], NT)
 
     def backward(key_slot, query_slot, valid, lse, delta, to_query, to_key, first=False):
         def block(t, carry):
@@ -451,15 +479,22 @@
     dqt[...] = jnp.zeros_like(dqt)
     arrived(attb.at[1 - c], r_core.at[4])
     rs_step(0, proj_part, 4)
+    q_round(2)
+    o_round(2)
+    s_round(2)
     backward(slot, slot, one, lse, delta, True, True, True)
     rs_step(0, proj_part, 3)
-    s_round(2)
     backward(slot_b, slot, key_tiles[1][1], lse, delta, True, False)
+    backward(slot_a, slot, key_tiles[2][1], lse, delta, True, False)
     rs_step(0, proj_part, 2)
     s_round(3)
-    backward(slot_a, slot, key_tiles[2][1], lse, delta, True, False)
+    q_round(3)
+    o_round(3)
+    s_round(4)
     rs_step(0, proj_part, 1)
-    s_round(4)
+    q_round(4)
+    o_round(4)
+    rs_finish(0, proj_part)
     q_round(5)
     o_round(5)
     s_round(5)
@@ -469,7 +504,6 @@
 
     s, valid = query_tiles[0]
     backward(slot, s, valid, from_stats(s, 0), from_stats(s, 8), False, True)
-    rs_finish(0, proj_part)
     s, valid = query_tiles[1]
     backward(slot, s, valid, from_stats(s, 0), from_stats(s, 8), False, True)
 
@@ -494,11 +528,10 @@
     arrived(dqb.at[1 - c], r_core.at[5])
     rs_step(1, dmod_part, 4)
     rs_step(1, dmod_part, 3)
+    ret_wait(0)
+    res_out[...] = (hid[...].astype(F32) + gate * ret[0].astype(F32)).astype(BF16)
     rs_step(1, dmod_part, 2)
     rs_step(1, dmod_part, 1)
-
-    ret_wait(0)
-    res_out[...] = (hid[...].astype(F32) + gate * ret[0].astype(F32)).astype(BF16)
     rs_finish(1, dmod_part)
     hat, r = normed()
     ret_wait(1)
@@ -532,9 +565,9 @@
             V((16, TILE, HD), BF16), V((16, TILE, HD), BF16), V((16, TILE, HD), BF16), V((16, TILE, HD), BF16),
             V((16, 16, HD), F32), V((2, TILE, HD), BF16), V((2, TILE, 384), BF16),
             V((HD, TILE), F32), V((HD, TILE), F32), V((TILE, HD), F32), V((TILE, HD), F32),
-            V((2, 2, 336, HALF), BF16), V((2, 2, 336, HALF), BF16), V((2, CH, HALF), BF16), V((2, SUB, D), BF16),
-            dma((2, 2)), dma((2, 2)), dma((2,)), dma((2,)), dma((2,)), dma((2, 8)), dma((2, 8)), dma((6,)), dma((6,)),
-            dma((5, 20)), dma((5, 20)), dma((2, 8)), dma((2, 8)), dma((2, 2)), dma((2, 2)),
+            V((2, 2, 336, HALF), BF16), V((2, 2, 336, HALF), BF16), V((2, CH, HALF), BF16), V((2, SUB, D), BF16), V((2 * CH, HALF), F32),
+            dma((2, 2)), dma((2, 2)), dma((2, 5)), dma((2, 5)), dma((2,)), dma((2, 16)), dma((2, 16)), dma((6,)), dma((6,)),
+            dma((5, 20)), dma((5, 20)), dma((2, 16)), dma((2, 16)), dma((2, 2)), dma((2, 2)),
         ],
         compiler_params=pltpu.CompilerParams(
             collective_id=0, has_side_effects=True, vmem_limit_bytes=60 * 2 ** 20

time: 199 us -> 175 us (0.88)
  Pallas kernels: 192 us -> 168 us
    pallas_call x1, Pallas kernels: 192 us -> 168 us  [per_device(): pl.pallas_call(kernel, out_shape=[jax.ShapeDtypeStruct(hidden.shape, BF16...]
where the time goes in v2:
time: 175 us
  Pallas kernels  168 us (96%)
  local copies, waits for them, and re-layouts  5.42 us (3%)
    pallas_call x1, Pallas kernels, per_device(): pl.pallas_call(kernel, out_shape=[jax.ShapeDtypeStruct(hidden.shape, BF16...  168 us
    unnamed x6, local copies, waits for them, and re-layouts  5.39 us

profile of v2, /device:TPU:9, one launch (start us, length us, event | category | flops | bytes accessed | tf_op | source)
XLA Modules:
  0.0 174.7 jit_solution(14586845306965251477)
XLA Ops:
  0.6 0.0 copy-start
  1.4 1.4 copy.12.pairs
  2.7 0.0 copy-done
  2.8 0.6 copy.15
  3.4 167.9 %sublayer.1 = (bf16[48,3072]{1,0:T(8,128)(2,1)}, bf16[48,3072]{1,0:T(8,128)(2,1)}) custom-call(bf16[48,3072]{1,0:T(8,128)(2,1)} %hid.1, bf16[48,3072]{1,0:T(8,128)(2,1)} %cot.1, f32[3,3072]{1,0:T(4,128)} %bitcast.11, bf16[3072,384]{1,0:T(8,128)(2,1)} %bitcast.9, f32[2,128]{1,0:T(2,128)} %gains.1, bf16[128,3072]{1,0:T(8,128)(2,1)} %bitcast.10, ...), custom_call_target="tpu_custom_call" | custom-call | tf_op jit(solution)/shard_map/sublayer/pallas_call | solution.py:556
  171.4 1.7 copy.19
  173.1 1.7 copy.20
  (1 shorter events, 0.0 us)
Async XLA Ops:
  0.6 2.1 %copy-start = (f32[32,3,3072]{2,0,1:T(8,128)S(1)}, f32[32,3,3072]{2,0,1:T(8,128)}, u32[]{:S(2)}) copy-start(f32[32,3,3072]{2,0,1:T(8,128)} %param.12) | copy-start | bytes 3538948

commit v3 on v2

--- a/solution.py
+++ b/solution.py
@@ -9,6 +9,7 @@
 
 EPS = 1e-6
 TILE = 768
+HALF_T = TILE // 2
 HD = 128
 D = 3072
 HALF = D // 2
@@ -34,6 +35,7 @@
     xs, cs, xg, cg, wq, wo, raw, psend, precv, dsend, drecv,
     qa, ka, va, doa, sta, attb, dqb, ot, dqt, dk, dv,
     rsnd, rrcv, rfin, ret, pbuf,
+    nk, nv, nq, no, gk, gv, gq, go_, near_s, far_s, inv,
     s_cross, r_cross, s_w, r_w, l_w, s_z, r_z, s_core, r_core,
     s_pl, r_pl, s_rs, r_rs, s_ret, r_ret,
 ):
@@ -82,6 +84,13 @@
     xs[...] = (hat * (1.0 + scale) + shift).astype(BF16)
     cs[...] = (cot[...].astype(F32) * gate).astype(BF16)
 
+    owners = [owner[(s // 4 * 2 + s % 2) * 2 + (s % 4) // 2] for s in range(16)]
+    for t in range(16):
+        found = jnp.int32(0)
+        for s in range(16):
+            found = jnp.where(owners[s] == t, s, found)
+        inv[t] = found
+
     pl.semaphore_wait(barrier, len(partners))
 
     def remote(src, dst, ss, rs, target):
@@ -161,13 +170,10 @@
     def w_quarter(n):
         arrived(w_view(n, 1 - yh, 0), r_w.at[n, 4])
 
-    send(wqkv.at[rows16(c * HALF + x * 384, 384)], w_view(0, yh, 0), s_w.at[0, 4], r_w.at[0, 4], wpartner)
     wq_local = pltpu.make_async_copy(wqkv.at[rows16(c * HALF, HALF)], wq.at[:, lanes(yh * 384, 384)], l_w.at[0])
     wo_local = pltpu.make_async_copy(wout.at[:, lanes(c * HALF, HALF)], wo.at[rows16(yh * HD, HD)], l_w.at[1])
     wq_local.start()
     wo_local.start()
-    cross_send(1, cs, cg)
-    send(wout.at[:, lanes(c * HALF + x * 384, 384)], w_view(1, yh, 0), s_w.at[1, 4], r_w.at[1, 4], wpartner)
 
     def z_piece(grid, off, h):
         return grid.at[rows_of(lax.rem(z + off + 16, 8), h)]
@@ -188,6 +194,9 @@
 
     cross_wait(0, xg)
     z_step(0, xg, 1)
+    send(wqkv.at[rows16(c * HALF + x * 384, 384)], w_view(0, yh, 0), s_w.at[0, 4], r_w.at[0, 4], wpartner)
+    cross_send(1, cs, cg)
+    send(wout.at[:, lanes(c * HALF + x * 384, 384)], w_view(1, yh, 0), s_w.at[1, 4], r_w.at[1, 4], wpartner)
     w_quarter(0)
     w_start(0, 0, 1)
     z_step(0, xg, 2)
@@ -230,9 +239,9 @@
         total = raw[r, :] + precv[r, :]
         raw[r, :] = total
         query, key = total[:, :HD], total[:, HD:2 * HD]
-        qa[slot, r, :] = (query * rms(query, 0)).astype(BF16)
-        ka[slot, r, :] = (key * rms(key, 1)).astype(BF16)
-        va[slot, r, :] = total[:, 2 * HD:].astype(BF16)
+        qa[x, r, :] = (query * rms(query, 0)).astype(BF16)
+        ka[x, r, :] = (key * rms(key, 1)).astype(BF16)
+        va[y, r, :] = total[:, 2 * HD:].astype(BF16)
         return carry
 
     lax.fori_loop(0, 3, norm_rows, 0)
@@ -293,11 +302,125 @@
                 wait(6, 7, 10, 11, 14, 15, 18, 19)
         return round_
 
-    k_round = plane(0, ka, TILE, False)
-    v_round = plane(1, va, TILE, True)
-    q_round = plane(2, qa, TILE, False)
-    o_round = plane(3, doa, TILE, True)
+    FIRST, LAST = pl.ds(0, HALF_T), pl.ds(HALF_T, HALF_T)
+
+    def neighbours(n, line, swap, mine, got, near, far):
+        a, b = (y, x) if swap else (x, y)
+
+        def target(axis, sign):
+            on_x = (axis == 0) != swap
+            return at_x(x + sign) if on_x else at_y(y + sign)
+
+        def need(step, role):
+            bb = lax.rem(b + step + 4, 4)
+            xx, yy = (bb, a) if swap else (a, bb)
+            tile = owner[(xx * 2 + lax.rem(yy, 2)) * 2 + yy // 2]
+            s = inv[lax.rem(tile + (15 if role == 0 else 1), 16)]
+            sx, sy = s // 4, lax.rem(s, 4)
+            return (sy, sx) if swap else (sx, sy)
+
+        def spot(off, part=None):
+            ref = line.at[lax.rem(a + off + 4, 4)]
+            return ref if part is None else ref.at[pl.ds(part * HALF_T, HALF_T)]
+
+        def go(i, src, dst, axis, sign):
+            send(src, dst, s_pl.at[n, i], r_pl.at[n, i], target(axis, sign))
+
+        def has(i, dst):
+            arrived(dst, r_pl.at[n, i])
+
+        def round_(k):
+            if k == 1:
+                go(0, spot(0), spot(0), 0, 1)
+                go(1, spot(0), spot(0), 0, -1)
+            elif k == 2:
+                has(0, spot(-1))
+                go(2, spot(-1, 0), spot(-1, 0), 0, 1)
+                has(1, spot(1))
+                go(3, spot(1, 1), spot(1, 1), 0, -1)
+            elif k == 3:
+                has(2, spot(-2, 0))
+                has(3, spot(2, 1))
+                for role in range(2):
+                    sa, _ = need(2, role)
+                    for side in range(2):
+                        far[0, role, side] = line[sa, pl.ds(side * HALF_T, HALF_T), :]
+                        go(4 + role * 2 + side, far.at[0, role, side], far.at[1, role, side], 1, -1 if side == 0 else 1)
+                for role in range(2):
+                    sa, _ = need(-1, role)
+                    near[0, role, LAST, :] = line[sa, LAST, :]
+                    go(8 + role * 2, near.at[0, role, LAST], got.at[0, role, LAST], 1, -1)
+                    sa, _ = need(1, role)
+                    near[1, role, FIRST, :] = line[sa, FIRST, :]
+                    go(9 + role * 2, near.at[1, role, FIRST], got.at[1, role, FIRST], 1, 1)
+            elif k == 4:
+                for role in range(2):
+                    for side, part in ((0, FIRST), (1, LAST)):
+                        sa, sb = need(-1 if side == 0 else 1, role)
+                        has(4 + role * 2 + side, far.at[1, role, side])
+                        near[side, role, part, :] = jnp.where(sb == b, line[sa, part, :], far[1, role, side])
+                        go(12 + role * 2 + side, near.at[side, role, part], got.at[side, role, part], 1, -1 if side == 0 else 1)
+            else:
+                for role in range(2):
+                    has(8 + role * 2, got.at[0, role, LAST])
+                    has(9 + role * 2, got.at[1, role, FIRST])
+                    has(12 + role * 2, got.at[0, role, FIRST])
+                    has(13 + role * 2, got.at[1, role, LAST])
+                for role in range(2):
+                    sa, sb = need(0, role)
+                    step = lax.rem(sb - b + 4, 4)
+                    up = jnp.where(jnp.logical_or(step == 1, step == 2), 0, 1)
+                    down = jnp.where(step >= 2, 1, 0)
+                    mine[role, FIRST, :] = jnp.where(step == 0, line[sa, FIRST, :], got[up, role, FIRST, :])
+                    mine[role, LAST, :] = jnp.where(step == 0, line[sa, LAST, :], got[down, role, LAST, :])
+        return round_
+
+    k_round = neighbours(0, ka, False, nk, gk, near_s.at[0], far_s.at[0])
+    v_round = neighbours(1, va, True, nv, gv, near_s.at[1], far_s.at[1])
+    q_round = neighbours(2, qa, False, nq, gq, near_s.at[2], far_s.at[2])
+    o_round = neighbours(3, doa, True, no, go_, near_s.at[3], far_s.at[3])
     s_round = plane(4, sta, 16, False)
+
+    tile = owner[(x * 2 + yl) * 2 + yh]
+    before = lax.rem(tile + 15, 16)
+    after = lax.rem(tile + 1, 16)
+    slot_b = inv[before]
+    slot_a = inv[after]
+
+    def lists(a, b):
+        hit = jnp.float32(0.0)
+        for n in range(3):
+            hit = jnp.where(pairs[a, n] == b, 1.0, hit)
+        return hit
+
+    one = jnp.float32(1.0)
+    own_k, own_v, own_q, own_o = ka.at[x], va.at[y], qa.at[x], doa.at[y]
+    key_tiles = [
+        (own_k, own_v, one),
+        (nk.at[0], nv.at[0], lists(tile, before)),
+        (nk.at[1], nv.at[1], lists(tile, after)),
+    ]
+    query_tiles = [
+        (nq.at[0], no.at[0], slot_b, lists(before, tile)),
+        (nq.at[1], no.at[1], slot_a, lists(after, tile)),
+    ]
+    EXPC = FACTOR * LOG2E
+
+    def scores(keys_, query_):
+        return dot(keys_, query_, NT) * EXPC
+
+    ot[...] = jnp.zeros_like(ot)
+    total = jnp.zeros((1, TILE), F32)
+
+    def attend(total, entry):
+        keys_, values_, valid = entry
+
+        def block(t, total):
+            r = pl.ds(pl.multiple_of(t * 256, 256), 256)
+            e = jnp.exp2(scores(keys_[r, :], own_q[...])) * valid
+            ot[...] += dot(values_[r, :], e.astype(BF16), TN)
+            return total + jnp.sum(e, axis=0, keepdims=True)
+        return lax.fori_loop(0, 3, block, total)
 
     k_round(1)
     v_round(1)
@@ -305,7 +428,11 @@
     k_round(2)
     v_round(2)
     z_step(1, cg, 3)
+    k_round(3)
+    v_round(3)
     z_step(1, cg, 4)
+    k_round(4)
+    v_round(4)
     w_wait(1, 2, 3)
     wo_local.wait()
     z_end(1, cg)
@@ -320,54 +447,9 @@
 
     lax.fori_loop(0, 3, grad_rows, 0)
     send(dsend, drecv.at[1], s_core.at[3], r_core.at[3], sibling)
-    k_round(3)
-    v_round(3)
+    total = attend(total, key_tiles[0])
     arrived(drecv.at[1], r_core.at[3])
-    doa[slot] = (drecv[0] + drecv[1]).astype(BF16)
-
-    def position(s):
-        return (s // 4 * 2 + s % 2) * 2 + (s % 4) // 2
-
-    tile = owner[(x * 2 + yl) * 2 + yh]
-    before = lax.rem(tile + 15, 16)
-    after = lax.rem(tile + 1, 16)
-    slot_b = jnp.int32(0)
-    slot_a = jnp.int32(0)
-    for s in range(16):
-        o = owner[position(s)]
-        slot_b = jnp.where(o == before, s, slot_b)
-        slot_a = jnp.where(o == after, s, slot_a)
-
-    def lists(a, b):
-        hit = jnp.float32(0.0)
-        for n in range(3):
-            hit = jnp.where(pairs[a, n] == b, 1.0, hit)
-        return hit
-
-    one = jnp.float32(1.0)
-    key_tiles = [(slot, one), (slot_b, lists(tile, before)), (slot_a, lists(tile, after))]
-    query_tiles = [(slot_b, lists(before, tile)), (slot_a, lists(after, tile))]
-    EXPC = FACTOR * LOG2E
-
-    def scores(keys_, query_):
-        return dot(keys_, query_, NT) * EXPC
-
-    ot[...] = jnp.zeros_like(ot)
-    total = jnp.zeros((1, TILE), F32)
-
-    def attend(total, entry):
-        s, valid = entry
-
-        def block(t, total):
-            r = pl.ds(pl.multiple_of(t * 256, 256), 256)
-            e = jnp.exp2(scores(ka[s, r, :], qa[slot])) * valid
-            ot[...] += dot(va[s, r, :], e.astype(BF16), TN)
-            return total + jnp.sum(e, axis=0, keepdims=True)
-        return lax.fori_loop(0, 3, block, total)
-
-    total = attend(total, key_tiles[0])
-    k_round(4)
-    v_round(4)
+    doa[y] = (drecv[0] + drecv[1]).astype(BF16)
     q_round(1)
     o_round(1)
     k_round(5)
@@ -378,7 +460,7 @@
     attb[c] = out_t.T.astype(BF16)
     send(attb.at[c], attb.at[c], s_core.at[4], r_core.at[4], sibling)
     lse = jnp.log2(total)
-    delta = jnp.sum(out_t * doa[slot].astype(F32).T, axis=0, keepdims=True)
+    delta = jnp.sum(out_t * own_o[...].astype(F32).T, axis=0, keepdims=True)
     for i in range(6):
         sta[slot, i:i + 1, :] = lse[:, i * HD:(i + 1) * HD]
         sta[slot, 8 + i:9 + i, :] = delta[:, i * HD:(i + 1) * HD]
@@ -453,14 +535,14 @@
     def dmod_part(spans):
         return dot(stack(dqb, spans), wq[...], NT)
 
-    def backward(key_slot, query_slot, valid, lse, delta, to_query, to_key, first=False):
+    def backward(kref, vref, qref, oref, valid, lse, delta, to_query, to_key, first=False):
         def block(t, carry):
             r = pl.ds(pl.multiple_of(t * 256, 256), 256)
-            keys_ = ka[key_slot, r, :]
-            query_ = qa[query_slot]
-            grad_ = doa[query_slot]
+            keys_ = kref[r, :]
+            query_ = qref[...]
+            grad_ = oref[...]
             p = jnp.exp2(scores(keys_, query_) - lse) * valid
-            d_prob = dot(va[key_slot, r, :], grad_, NT)
+            d_prob = dot(vref[r, :], grad_, NT)
             ds = (p * (d_prob - delta)).astype(BF16)
             if to_query:
                 dqt[...] += dot(keys_, ds, TN)
@@ -481,20 +563,19 @@
     rs_step(0, proj_part, 4)
     q_round(2)
     o_round(2)
-    s_round(2)
-    backward(slot, slot, one, lse, delta, True, True, True)
-    rs_step(0, proj_part, 3)
-    backward(slot_b, slot, key_tiles[1][1], lse, delta, True, False)
-    backward(slot_a, slot, key_tiles[2][1], lse, delta, True, False)
-    rs_step(0, proj_part, 2)
-    s_round(3)
     q_round(3)
     o_round(3)
-    s_round(4)
-    rs_step(0, proj_part, 1)
+    s_round(2)
+    rs_step(0, proj_part, 3)
+    backward(own_k, own_v, own_q, own_o, one, lse, delta, True, True, True)
+    s_round(3)
+    rs_step(0, proj_part, 2)
+    backward(nk.at[0], nv.at[0], own_q, own_o, key_tiles[1][2], lse, delta, True, False)
     q_round(4)
     o_round(4)
-    rs_finish(0, proj_part)
+    s_round(4)
+    backward(nk.at[1], nv.at[1], own_q, own_o, key_tiles[2][2], lse, delta, True, False)
+    rs_step(0, proj_part, 1)
     q_round(5)
     o_round(5)
     s_round(5)
@@ -502,10 +583,11 @@
     def from_stats(s, first):
         return jnp.concatenate([sta[s, first + i:first + i + 1, :] for i in range(6)], axis=1)
 
-    s, valid = query_tiles[0]
-    backward(slot, s, valid, from_stats(s, 0), from_stats(s, 8), False, True)
-    s, valid = query_tiles[1]
-    backward(slot, s, valid, from_stats(s, 0), from_stats(s, 8), False, True)
+    q_, o_, s, valid = query_tiles[0]
+    backward(own_k, own_v, q_, o_, valid, from_stats(s, 0), from_stats(s, 8), False, True)
+    q_, o_, s, valid = query_tiles[1]
+    backward(own_k, own_v, q_, o_, valid, from_stats(s, 0), from_stats(s, 8), False, True)
+    rs_finish(0, proj_part)
 
     def through_norm(source, grad, row):
         r = lax.rsqrt(jnp.mean(source * source, axis=-1, keepdims=True) + EPS)
@@ -562,10 +644,12 @@
             V((SUB, D), BF16), V((SUB, D), BF16), V((TILE, HALF), BF16), V((TILE, HALF), BF16),
             V((HALF, 768), BF16), V((256, HALF), BF16), V((TILE, 384), F32), V((TILE, 384), F32), V((TILE, 384), F32),
             V((TILE, HD), F32), V((2, TILE, HD), F32),
-            V((16, TILE, HD), BF16), V((16, TILE, HD), BF16), V((16, TILE, HD), BF16), V((16, TILE, HD), BF16),
+            *[V((4, TILE, HD), BF16)] * 4,
             V((16, 16, HD), F32), V((2, TILE, HD), BF16), V((2, TILE, 384), BF16),
             V((HD, TILE), F32), V((HD, TILE), F32), V((TILE, HD), F32), V((TILE, HD), F32),
             V((2, 2, 336, HALF), BF16), V((2, 2, 336, HALF), BF16), V((2, CH, HALF), BF16), V((2, SUB, D), BF16), V((2 * CH, HALF), F32),
+            *[V((2, TILE, HD), BF16)] * 4, *[V((2, 2, TILE, HD), BF16)] * 4,
+            V((4, 2, 2, TILE, HD), BF16), V((4, 2, 2, 2, HALF_T, HD), BF16), pltpu.SMEM((16,), jnp.int32),
             dma((2, 2)), dma((2, 2)), dma((2, 5)), dma((2, 5)), dma((2,)), dma((2, 16)), dma((2, 16)), dma((6,)), dma((6,)),
             dma((5, 20)), dma((5, 20)), dma((2, 16)), dma((2, 16)), dma((2, 2)), dma((2, 2)),
         ],

time: 175 us -> 163 us (0.931); the launches traced: 175 us -> 160 us
  Pallas kernels: 168 us -> 153 us
    pallas_call x1, Pallas kernels: 168 us -> 153 us  [per_device(): pl.pallas_call(kernel, out_shape=[jax.ShapeDtypeStruct(hidden.shape, BF16...]
where the time goes in v3:
time: 163 us; the launch traced here: 160 us
  Pallas kernels  153 us (94%)
  local copies, waits for them, and re-layouts  5.42 us (3%)
    pallas_call x1, Pallas kernels, per_device(): pl.pallas_call(kernel, out_shape=[jax.ShapeDtypeStruct(hidden.shape, BF16...  153 us
    unnamed x6, local copies, waits for them, and re-layouts  5.39 us

profile of v3, /device:TPU:9, one launch (start us, length us, event | category | flops | bytes accessed | tf_op | source)
XLA Modules:
  0.0 160.1 jit_solution(3872467771589631253)
XLA Ops:
  0.6 0.0 copy-start
  1.4 1.4 copy.12.pairs
  2.7 0.0 copy-done
  2.8 0.6 copy.15
  3.4 153.2 %sublayer.1 = (bf16[48,3072]{1,0:T(8,128)(2,1)}, bf16[48,3072]{1,0:T(8,128)(2,1)}) custom-call(bf16[48,3072]{1,0:T(8,128)(2,1)} %hid.1, bf16[48,3072]{1,0:T(8,128)(2,1)} %cot.1, f32[3,3072]{1,0:T(4,128)} %bitcast.11, bf16[3072,384]{1,0:T(8,128)(2,1)} %bitcast.9, f32[2,128]{1,0:T(2,128)} %gains.1, bf16[128,3072]{1,0:T(8,128)(2,1)} %bitcast.10, ...), custom_call_target="tpu_custom_call" | custom-call | tf_op jit(solution)/shard_map/sublayer/pallas_call | solution.py:638
  156.7 1.7 %copy.19 = bf16[48,3072]{1,0:T(8,128)(2,1)} copy(bf16[48,3072]{1,0:T(8,128)(2,1)} %get-tuple-element.4) | data formatting | bytes 589824
  158.4 1.7 %copy.20 = bf16[48,3072]{1,0:T(8,128)(2,1)} copy(bf16[48,3072]{1,0:T(8,128)(2,1)} %get-tuple-element.5) | data formatting | bytes 589824
  (1 shorter events, 0.0 us)
Async XLA Ops:
  0.6 2.1 %copy-start = (f32[32,3,3072]{2,0,1:T(8,128)S(1)}, f32[32,3,3072]{2,0,1:T(8,128)}, u32[]{:S(2)}) copy-start(f32[32,3,3072]{2,0,1:T(8,128)} %param.12) | copy-start | bytes 3538948

commit v4 on v3

--- a/solution.py
+++ b/solution.py
@@ -30,7 +30,7 @@
 
 
 def kernel(
-    hid, cot, mods, wqkv, gains, wout, pairs, owner,
+    hid, cot, step_ref, modt, wqkv, gains, wout, pairs, owner,
     res_out, gh_out,
     xs, cs, xg, cg, wq, wo, raw, psend, precv, dsend, drecv,
     qa, ka, va, doa, sta, attb, dqb, ot, dqt, dk, dv,
@@ -69,9 +69,10 @@
     for p in partners:
         pl.semaphore_signal(barrier, inc=1, device_id=p, device_id_type=MESH)
 
-    shift = mods[0:1, :]
-    scale = mods[1:2, :]
-    gate = mods[2:3, :]
+    step = step_ref[0]
+    shift = modt[0, pl.ds(step, 1), :]
+    scale = modt[1, pl.ds(step, 1), :]
+    gate = modt[2, pl.ds(step, 1), :]
 
     def normed():
         rows = hid[...].astype(F32)
@@ -134,12 +135,12 @@
                     copy.wait_send()
             pending.append(done)
 
-    def cross_wait(n, grid):
-        for sub in range(2):
-            dst = grid.at[rows_of(z, sub)]
-            pltpu.make_async_copy(dst, dst, r_cross.at[n, sub]).wait()
+    def cross_wait(n, grid, sub):
+        dst = grid.at[rows_of(z, sub)]
+        pltpu.make_async_copy(dst, dst, r_cross.at[n, sub]).wait()
 
     cross_send(0, xs, xg)
+
     def lanes(first, size):
         return pl.ds(pl.multiple_of(first, 128), size)
 
@@ -179,7 +180,9 @@
         return grid.at[rows_of(lax.rem(z + off + 16, 8), h)]
 
     def z_step(n, grid, j):
-        for h in range(2):
+        for h in (yh, 1 - yh) if j < 4 else (0, 1):
+            if j == 1:
+                cross_wait(n, grid, h)
             for i, sign in enumerate((1, -1)):
                 if j > 1:
                     arrived(z_piece(grid, -sign * (j - 1), h), r_z.at[n, (j - 2) * 4 + i * 2 + h])
@@ -192,24 +195,22 @@
         for i, sign in enumerate((1, -1)):
             arrived(z_piece(grid, -sign * 4, i), r_z.at[n, 12 + i * 3])
 
-    cross_wait(0, xg)
     z_step(0, xg, 1)
     send(wqkv.at[rows16(c * HALF + x * 384, 384)], w_view(0, yh, 0), s_w.at[0, 4], r_w.at[0, 4], wpartner)
     cross_send(1, cs, cg)
     send(wout.at[:, lanes(c * HALF + x * 384, 384)], w_view(1, yh, 0), s_w.at[1, 4], r_w.at[1, 4], wpartner)
+    z_step(0, xg, 2)
     w_quarter(0)
     w_start(0, 0, 1)
-    z_step(0, xg, 2)
-    cross_wait(1, cg)
+    z_step(0, xg, 3)
     w_quarter(1)
     w_start(1, 0, 1)
-    z_step(0, xg, 3)
     w_wait(0, 0, 1)
     w_start(0, 2, 3)
+    z_step(0, xg, 4)
+    z_step(1, cg, 1)
     w_wait(1, 0, 1)
     w_start(1, 2, 3)
-    z_step(0, xg, 4)
-    z_step(1, cg, 1)
     w_wait(0, 2, 3)
     wq_local.wait()
     z_end(0, xg)
@@ -390,7 +391,7 @@
     def lists(a, b):
         hit = jnp.float32(0.0)
         for n in range(3):
-            hit = jnp.where(pairs[a, n] == b, 1.0, hit)
+            hit = jnp.where(pairs[n, a] == b, 1.0, hit)
         return hit
 
     one = jnp.float32(1.0)
@@ -633,12 +634,11 @@
     sm = pl.BlockSpec(memory_space=pltpu.SMEM)
     hbm = pl.BlockSpec(memory_space=pl.ANY)
     dma = pltpu.SemaphoreType.DMA
-    mods = lax.dynamic_index_in_dim(mod_table, step_index[0], 0, keepdims=False)
     V = pltpu.VMEM
     return pl.pallas_call(
         kernel,
         out_shape=[jax.ShapeDtypeStruct(hidden.shape, BF16)] * 2,
-        in_specs=[vm, vm, vm, hbm, vm, hbm, sm, sm],
+        in_specs=[vm, vm, sm, vm, hbm, vm, hbm, sm, sm],
         out_specs=[vm, vm],
         scratch_shapes=[
             V((SUB, D), BF16), V((SUB, D), BF16), V((TILE, HALF), BF16), V((TILE, HALF), BF16),
@@ -658,8 +658,8 @@
         ),
         name="sublayer",
     )(
-        hidden, cotangent, mods, w_qkv.reshape(D, 384),
-        qk_gains, w_out.reshape(HD, D), tile_pairs, tile_owner,
+        hidden, cotangent, step_index, jnp.transpose(mod_table, (1, 0, 2)), w_qkv.reshape(D, 384),
+        qk_gains, w_out.reshape(HD, D), tile_pairs.T, tile_owner,
     )
 
 

time: 163 us -> 154 us (0.945)
  Pallas kernels: 153 us -> 148 us
  local copies, waits for them, and re-layouts: 5.42 us -> 3.39 us
    pallas_call x1, Pallas kernels: 153 us -> 148 us  [per_device(): pl.pallas_call(kernel, out_shape=[jax.ShapeDtypeStruct(hidden.shape, BF16...]
    unnamed x6 -> x2, local copies, waits for them, and re-layouts: 5.39 us -> 3.39 us
where the time goes in v4:
time: 154 us; the launch traced here: 153 us
  Pallas kernels  148 us (96%)
  local copies, waits for them, and re-layouts  3.39 us (2%)
    pallas_call x1, Pallas kernels, per_device(): pl.pallas_call(kernel, out_shape=[jax.ShapeDtypeStruct(hidden.shape, BF16...  148 us
    unnamed x2, local copies, waits for them, and re-layouts  3.39 us

profile of v4, /device:TPU:9, one launch (start us, length us, event | category | flops | bytes accessed | tf_op | source)
XLA Modules:
  0.0 152.6 jit_solution(17823414630250286487)
XLA Ops:
  1.3 147.9 %sublayer.1 = (bf16[48,3072]{1,0:T(8,128)(2,1)}, bf16[48,3072]{1,0:T(8,128)(2,1)}) custom-call(bf16[48,3072]{1,0:T(8,128)(2,1)} %hid.1, bf16[48,3072]{1,0:T(8,128)(2,1)} %cot.1, s32[1]{0:T(128)S(6)} %copy.13.step_ref, f32[3,32,3072]{2,1,0:T(8,128)} %bitcast.5, bf16[3072,384]{1,0:T(8,128)(2,1)} %bitcast.4, f32[2,128]{1,0:T(2,128)} %gains.1, ...), custom_call_target="tpu_custom_call" | custom-call | tf_op jit(solution)/shard_map/sublayer/pallas_call | solution.py:638
  149.2 1.7 %copy.14 = bf16[48,3072]{1,0:T(8,128)(2,1)} copy(bf16[48,3072]{1,0:T(8,128)(2,1)} %get-tuple-element.4) | data formatting | bytes 589824
  150.9 1.7 %copy.15 = bf16[48,3072]{1,0:T(8,128)(2,1)} copy(bf16[48,3072]{1,0:T(8,128)(2,1)} %get-tuple-element.5) | data formatting | bytes 589824

commit v5 on v4

--- a/solution.py
+++ b/solution.py
@@ -456,6 +456,8 @@
     k_round(5)
     v_round(5)
     total = attend(total, key_tiles[1])
+    q_round(2)
+    o_round(2)
     total = attend(total, key_tiles[2])
     out_t = (ot[...] / total).astype(BF16).astype(F32)
     attb[c] = out_t.T.astype(BF16)
@@ -491,15 +493,14 @@
 
     def rs_finish(n, partial):
         pbuf[:CH, :] = partial([rows_of(z, 0, CH)])
-        for h in range(2):
-            value = pbuf[h * SUB:(h + 1) * SUB, :]
-            r = pl.ds(base[1] + h * SUB, SUB)
-            for i in range(2):
-                arrived(rrcv.at[n, i, r], r_rs.at[n, i * 2 + h])
-                value = value + rrcv[n, i, r, :].astype(F32)
-            rfin[n, h * SUB:(h + 1) * SUB, :] = value.astype(BF16)
         cols = pl.ds(pl.multiple_of(c * HALF, 128), HALF)
         for sub in range(2):
+            value = pbuf[sub * SUB:(sub + 1) * SUB, :]
+            r = pl.ds(base[1] + sub * SUB, SUB)
+            for i in range(2):
+                arrived(rrcv.at[n, i, r], r_rs.at[n, i * 2 + sub])
+                value = value + rrcv[n, i, r, :].astype(F32)
+            rfin[n, sub * SUB:(sub + 1) * SUB, :] = value.astype(BF16)
             src = rfin.at[n, pl.ds(sub * SUB, SUB)]
             dst = ret.at[n, :, cols]
             here = jnp.logical_and(own, yh == sub)
@@ -562,18 +563,16 @@
     dqt[...] = jnp.zeros_like(dqt)
     arrived(attb.at[1 - c], r_core.at[4])
     rs_step(0, proj_part, 4)
-    q_round(2)
-    o_round(2)
     q_round(3)
     o_round(3)
     s_round(2)
+    backward(own_k, own_v, own_q, own_o, one, lse, delta, True, True, True)
     rs_step(0, proj_part, 3)
-    backward(own_k, own_v, own_q, own_o, one, lse, delta, True, True, True)
-    s_round(3)
-    rs_step(0, proj_part, 2)
-    backward(nk.at[0], nv.at[0], own_q, own_o, key_tiles[1][2], lse, delta, True, False)
     q_round(4)
     o_round(4)
+    s_round(3)
+    backward(nk.at[0], nv.at[0], own_q, own_o, key_tiles[1][2], lse, delta, True, False)
+    rs_step(0, proj_part, 2)
     s_round(4)
     backward(nk.at[1], nv.at[1], own_q, own_o, key_tiles[2][2], lse, delta, True, False)
     rs_step(0, proj_part, 1)

time: 154 us -> 151 us (0.981)
  Pallas kernels: 148 us -> 144 us
    pallas_call x1, Pallas kernels: 148 us -> 144 us  [per_device(): pl.pallas_call(kernel, out_shape=[jax.ShapeDtypeStruct(hidden.shape, BF16...]
where the time goes in v5:
time: 151 us; the launch traced here: 149 us
  Pallas kernels  144 us (95%)
  local copies, waits for them, and re-layouts  3.39 us (2%)
    pallas_call x1, Pallas kernels, per_device(): pl.pallas_call(kernel, out_shape=[jax.ShapeDtypeStruct(hidden.shape, BF16...  144 us
    unnamed x2, local copies, waits for them, and re-layouts  3.39 us

profile of v5, /device:TPU:9, one launch (start us, length us, event | category | flops | bytes accessed | tf_op | source)
XLA Modules:
  0.0 148.8 jit_solution(18022302985496763759)
XLA Ops:
  1.3 144.2 %sublayer.1 = (bf16[48,3072]{1,0:T(8,128)(2,1)}, bf16[48,3072]{1,0:T(8,128)(2,1)}) custom-call(bf16[48,3072]{1,0:T(8,128)(2,1)} %hid.1, bf16[48,3072]{1,0:T(8,128)(2,1)} %cot.1, s32[1]{0:T(128)S(6)} %copy.13.step_ref, f32[3,32,3072]{2,1,0:T(8,128)} %bitcast.5, bf16[3072,384]{1,0:T(8,128)(2,1)} %bitcast.4, f32[2,128]{1,0:T(2,128)} %gains.1, ...), custom_call_target="tpu_custom_call" | custom-call | tf_op jit(solution)/shard_map/sublayer/pallas_call | solution.py:637
  145.5 1.7 %copy.14 = bf16[48,3072]{1,0:T(8,128)(2,1)} copy(bf16[48,3072]{1,0:T(8,128)(2,1)} %get-tuple-element.4) | data formatting | bytes 589824
  147.2 1.7 %copy.15 = bf16[48,3072]{1,0:T(8,128)(2,1)} copy(bf16[48,3072]{1,0:T(8,128)(2,1)} %get-tuple-element.5) | data formatting | bytes 589824
